TPU v7x, 128 devices: a whole 4x4x4 slice. The times are simulated.
128 devices in a mesh: section: 4 (over y), expert: 32 (over z, x, core).
Axes of the slice: x: 4, y: 4, z: 4, core: 2. Of those that a mesh axis runs over, the one named last changes fastest.
Arguments:
- tokens: bfloat16 [4, 256, 3584], P('section', 'expert'), may hold values from -6 to 6
- norm_gain: bfloat16 [4, 3584], P('section'), may hold values from 0.5 to 1.5
- router: bfloat16 [4, 3584, 32], P('section'), may hold values from -0.09375 to 0.09375
- w_gate: bfloat16 [4, 32, 3584, 1024], P('section', 'expert'), may hold values from -0.09375 to 0.09375
- w_up: bfloat16 [4, 32, 3584, 1024], P('section', 'expert'), may hold values from -0.09375 to 0.09375
- w_down: bfloat16 [4, 32, 1024, 3584], P('section', 'expert'), may hold values from -0.1875 to 0.1875
- expert_ids: int32 [4, 4, 256, 8], P('section', None, 'expert'), may hold values from 0 to 31, all different within a row
Outputs:
- mixed: bfloat16 [4, 256, 3584], P('section', 'expert')
Inputs may be any that keep to these rules, and one draw needn't show every extreme that they name: `expert_ids`: each row names 8 different experts.
All inputs are finite; a program needn't handle non-finite values.
Results may differ from a plain program's by a relative error of at most 0.022.
Values may be sent and summed in bfloat16 or wider, within the bound.
A program may use at most 128 MiB of HBM per device.

v0:
```python
import jax
import jax.numpy as jnp
from jax import lax
from jax.sharding import PartitionSpec as P

epsilon = 1e-06
routed_scale = 2.5


def passed_along(block, axis, distance):
    devices = range(lax.axis_size(axis))
    route = [(i - distance, i) for i in devices if i - distance in devices]
    return lax.ppermute(block, axis, route)


def normalize(hidden_rows, gain_row):
    values = hidden_rows.astype(jnp.float32)
    inverse_rms = lax.rsqrt(jnp.mean(values * values, axis=-1, keepdims=True) + epsilon)
    return (values * inverse_rms * gain_row.astype(jnp.float32)).astype(jnp.bfloat16)


def route(normed, choices, router_cols, blocks):
    expert_count = router_cols.shape[1]
    logits = jnp.dot(normed, router_cols, preferred_element_type=jnp.float32)
    scores = jax.nn.sigmoid(logits)
    onehot = choices[:, :, None] == jnp.arange(expert_count, dtype=jnp.int32)[None, None, :]
    picked = jnp.sum(jnp.where(onehot, scores[:, None, :], 0.0), axis=-1)
    weights = routed_scale * picked / jnp.sum(picked, axis=-1, keepdims=True)
    indicator = onehot.astype(jnp.int32).reshape(blocks, -1, expert_count)
    earlier = jnp.cumsum(indicator, axis=1) - indicator
    positions = jnp.sum(earlier * indicator, axis=-1).reshape(choices.shape)
    return (weights, positions)


def expert_mlp(inputs, gate_weight, up_weight, down_weight):
    gate_part = jnp.dot(inputs, gate_weight, preferred_element_type=jnp.float32)
    up_part = jnp.dot(inputs, up_weight, preferred_element_type=jnp.float32)
    hidden = (jax.nn.silu(gate_part) * up_part).astype(jnp.bfloat16)
    return jnp.dot(hidden, down_weight, preferred_element_type=jnp.float32).astype(jnp.bfloat16)


def fill_slots(normed, slot_keys, total_slots):
    matches = slot_keys.reshape(-1)[None, :] == jnp.arange(total_slots, dtype=jnp.int32)[:, None]
    owners = jnp.arange(slot_keys.size, dtype=jnp.int32) // slot_keys.shape[1]
    source = jnp.sum(jnp.where(matches, owners[None, :], 0), axis=1)
    present = jnp.any(matches, axis=1)
    return jnp.where(present[:, None], normed[source], jnp.zeros((), jnp.bfloat16))


def send_back(produced):
    return lax.all_to_all(produced, "expert", split_axis=0, concat_axis=0, tiled=True)


def combine(hidden_rows, weights, positions, choices, capacity, returned):
    retained = positions < capacity
    slot_keys = jnp.where(retained, choices * capacity + positions, 0)
    picked = returned.reshape(-1, returned.shape[-1])[slot_keys]
    factor = jnp.where(retained, weights, 0.0)
    branch = jnp.einsum("tk,tkd->td", factor, picked.astype(jnp.float32))
    return (hidden_rows.astype(jnp.float32) + branch).astype(jnp.bfloat16)


def per_device(tokens, norm_gain, router, w_gate, w_up, w_down, expert_ids):
    sections = lax.axis_size("section")
    section_index = lax.axis_index("section")
    expert_count = lax.axis_size("expert")
    owner_index = lax.axis_index("expert")
    micro_count = expert_ids.shape[1]
    row_count = tokens.shape[1]
    model_width = tokens.shape[2]
    top_count = expert_ids.shape[3]
    capacity = min(row_count, max(2, 5 * row_count * top_count // (4 * expert_count)))
    gate_weight = w_gate[0, 0]
    up_weight = w_up[0, 0]
    down_weight = w_down[0, 0]
    gain_row = norm_gain[0]
    router_cols = router[0]
    every_ids = lax.all_gather(expert_ids, "expert", axis=2, tiled=True)
    holding = tokens[0]
    current = jnp.zeros_like(holding)
    total_steps = sections + micro_count - 1
    for moment in range(total_steps):
        if moment > 0:
            holding = passed_along(holding, "section", -1)
        incoming = jnp.where(section_index == 0, holding, current)
        micro_index = jnp.clip(moment - section_index, 0, micro_count - 1)
        local_ids = lax.dynamic_index_in_dim(expert_ids[0], micro_index, 0, keepdims=False)
        normed = normalize(incoming, gain_row)
        all_ids = lax.dynamic_index_in_dim(every_ids[0], micro_index, 0, keepdims=False)
        everyone = lax.all_gather(normed, "expert", axis=0, tiled=True)
        all_weights, all_positions = route(everyone, all_ids, router_cols, expert_count)
        source_block = (jnp.arange(all_ids.shape[0], dtype=jnp.int32) // row_count)[:, None]
        wanted = (all_ids == owner_index) & (all_positions < capacity)
        slot_keys = jnp.where(wanted, source_block * capacity + all_positions, -1)
        arrived = fill_slots(everyone, slot_keys, expert_count * capacity)
        produced = expert_mlp(arrived, gate_weight, up_weight, down_weight)
        returned = send_back(produced.reshape(expert_count, capacity, model_width))
        weights = lax.dynamic_slice_in_dim(all_weights, owner_index * row_count, row_count, 0)
        positions = lax.dynamic_slice_in_dim(all_positions, owner_index * row_count, row_count, 0)
        result = combine(incoming, weights, positions, local_ids, capacity, returned)
        finished = (section_index == sections - 1) & (moment - section_index >= 0)
        holding = jnp.where(finished, result, holding)
        if moment < total_steps - 1:
            current = passed_along(result, "section", 1)
    return holding[None]


def solution(mesh):
    placed = (
        P("section", "expert", None),
        P("section", None),
        P("section", None, None),
        P("section", "expert", None, None),
        P("section", "expert", None, None),
        P("section", "expert", None, None),
        P("section", None, "expert", None),
    )
    return jax.shard_map(
        per_device,
        mesh=mesh,
        in_specs=placed,
        out_specs=P("section", "expert", None),
        check_vma=False,
    )
```

profile of v0, /device:TPU:24, one launch (start us, length us, event | category | flops | bytes accessed | tf_op | source)
XLA Modules:
  0.0 613.4 jit_solution(815563225013542174)
XLA Ops:
  10.6 26.2 %all_gather.24 = s32[1,4,256,8]{3,1,0,2:T(4,128)S(1)} all-gather(s32[1,4,8,8]{3,1,0,2:T(4,128)S(1)} %copy.177), channel_id=1, replica_groups=mesh['section'=4,'expert'=32] {'expert'}, dimensions={2}, use_global_device_ids=true | all-gather | bytes 33792 | tf_op jit(solution)/shard_map/all_gather | solution.py:78
  64.0 4.5 fusion.40
  68.6 8.0 %fusion.42 = bf16[64,3584]{1,0:T(8,128)(2,1)S(1)} fusion(bf16[1,1,1024,3584]{3,2,1,0:T(8,128)(2,1)} %param.12, bf16[1,1,3584,1024]{3,2,1,0:T(8,128)(2,1)} %param.11, f32[64,1024]{1,0:T(8,128)S(1)} %fusion.40, bf16[64,3584]{1,0:T(8,128)(2,1)S(1)} %gather_fusion, pred[64]{0:T(512)(128)(4,1)S(1)} %fusion.180), kind=kOutput, calls=%fused_computation.56 | convolution fusion | flops 940376064 | bytes 15859776 | tf_op jit(solution)/shard_map/dot_general | solution.py:39
  77.6 5.1 all-to-all-start
  83.8 10.0 %all-to-all-done = bf16[32,2,3584]{2,1,0:T(2,128)(2,1)S(1)} async-done(((bf16[32,2,3584]{2,1,0:T(2,128)(2,1)}), bf16[32,2,3584]{2,1,0:T(2,128)(2,1)S(1)}, u32[]{:S(2)}, u32[]{:S(2)}) %all-to-all-start) | async-done | bytes 458784 | tf_op jit(solution)/shard_map/all_to_all | solution.py:51
  105.6 40.4 %all-gather.10.cloned.1.call-done = bf16[256,3584]{1,0:T(8,128)(2,1)} async-done(((bf16[8,3584]{1,0:T(8,128)(2,1)}), bf16[256,3584]{1,0:T(8,128)(2,1)}) %all-gather.10.cloned.1.call-update) | async-done | bytes 1835024 | tf_op jit(solution)/shard_map/all_gather | solution.py:90
  153.5 8.0 %fusion.45 = bf16[64,3584]{1,0:T(8,128)(2,1)S(1)} fusion(bf16[1,1,1024,3584]{3,2,1,0:T(8,128)(2,1)} %param.12, bf16[1,1,3584,1024]{3,2,1,0:T(8,128)(2,1)} %param.11, f32[64,1024]{1,0:T(8,128)S(1)} %fusion.38, bf16[64,3584]{1,0:T(8,128)(2,1)S(1)} %gather_fusion.2, pred[64]{0:T(512)(128)(4,1)S(1)} %fusion.178), kind=kOutput, calls=%fused_computation.57 | convolution fusion | flops 940376064 | bytes 15859776 | tf_op jit(solution)/shard_map/dot_general | solution.py:39
  162.5 5.2 all-to-all-start.1
  168.8 10.0 %all-to-all-done.1 = bf16[32,2,3584]{2,1,0:T(2,128)(2,1)S(1)} async-done(((bf16[32,2,3584]{2,1,0:T(2,128)(2,1)}), bf16[32,2,3584]{2,1,0:T(2,128)(2,1)S(1)}, u32[]{:S(2)}, u32[]{:S(2)}) %all-to-all-start.1) | async-done | bytes 458784 | tf_op jit(solution)/shard_map/all_to_all | solution.py:51
  190.1 40.9 %all-gather.12.cloned.1.call-done = bf16[256,3584]{1,0:T(8,128)(2,1)} async-done(((bf16[8,3584]{1,0:T(8,128)(2,1)}), bf16[256,3584]{1,0:T(8,128)(2,1)}) %all-gather.12.cloned.1.call-update) | async-done | bytes 1835024 | tf_op jit(solution)/shard_map/all_gather | solution.py:90
  234.0 4.5 fusion.36
  238.6 8.0 %fusion.48 = bf16[64,3584]{1,0:T(8,128)(2,1)S(1)} fusion(bf16[1,1,1024,3584]{3,2,1,0:T(8,128)(2,1)} %param.12, bf16[1,1,3584,1024]{3,2,1,0:T(8,128)(2,1)} %param.11, f32[64,1024]{1,0:T(8,128)S(1)} %fusion.36, bf16[64,3584]{1,0:T(8,128)(2,1)S(1)} %gather_fusion.4, pred[64]{0:T(512)(128)(4,1)S(1)} %fusion.176), kind=kOutput, calls=%fused_computation.58 | convolution fusion | flops 940376064 | bytes 15859776 | tf_op jit(solution)/shard_map/dot_general | solution.py:39
  247.6 5.2 all-to-all-start.2
  254.0 9.8 %all-to-all-done.2 = bf16[32,2,3584]{2,1,0:T(2,128)(2,1)S(1)} async-done(((bf16[32,2,3584]{2,1,0:T(2,128)(2,1)}), bf16[32,2,3584]{2,1,0:T(2,128)(2,1)S(1)}, u32[]{:S(2)}, u32[]{:S(2)}) %all-to-all-start.2) | async-done | bytes 458784 | tf_op jit(solution)/shard_map/all_to_all | solution.py:51
  275.7 40.4 %all-gather.14.cloned.1.call-done = bf16[256,3584]{1,0:T(8,128)(2,1)} async-done(((bf16[8,3584]{1,0:T(8,128)(2,1)}), bf16[256,3584]{1,0:T(8,128)(2,1)}) %all-gather.14.cloned.1.call-update) | async-done | bytes 1835024 | tf_op jit(solution)/shard_map/all_gather | solution.py:90
  319.1 4.5 fusion.34
  323.7 8.0 %fusion.51 = bf16[64,3584]{1,0:T(8,128)(2,1)S(1)} fusion(bf16[1,1,1024,3584]{3,2,1,0:T(8,128)(2,1)} %param.12, bf16[1,1,3584,1024]{3,2,1,0:T(8,128)(2,1)} %param.11, f32[64,1024]{1,0:T(8,128)S(1)} %fusion.34, bf16[64,3584]{1,0:T(8,128)(2,1)S(1)} %gather_fusion.6, pred[64]{0:T(512)(128)(4,1)S(1)} %fusion.174), kind=kOutput, calls=%fused_computation.59 | convolution fusion | flops 940376064 | bytes 15859776 | tf_op jit(solution)/shard_map/dot_general | solution.py:39
  332.7 5.2 all-to-all-start.3
  338.9 10.0 %all-to-all-done.3 = bf16[32,2,3584]{2,1,0:T(2,128)(2,1)S(1)} async-done(((bf16[32,2,3584]{2,1,0:T(2,128)(2,1)}), bf16[32,2,3584]{2,1,0:T(2,128)(2,1)S(1)}, u32[]{:S(2)}, u32[]{:S(2)}) %all-to-all-start.3) | async-done | bytes 458784 | tf_op jit(solution)/shard_map/all_to_all | solution.py:51
  360.2 40.9 %all-gather.16.cloned.1.call-done = bf16[256,3584]{1,0:T(8,128)(2,1)} async-done(((bf16[8,3584]{1,0:T(8,128)(2,1)}), bf16[256,3584]{1,0:T(8,128)(2,1)}) %all-gather.16.cloned.1.call-update) | async-done | bytes 1835024 | tf_op jit(solution)/shard_map/all_gather | solution.py:90
  408.7 8.0 %fusion.54 = bf16[64,3584]{1,0:T(8,128)(2,1)S(1)} fusion(bf16[1,1,1024,3584]{3,2,1,0:T(8,128)(2,1)} %param.12, bf16[1,1,3584,1024]{3,2,1,0:T(8,128)(2,1)} %param.11, f32[64,1024]{1,0:T(8,128)S(1)} %fusion.32, bf16[64,3584]{1,0:T(8,128)(2,1)S(1)} %gather_fusion.8, pred[64]{0:T(512)(128)(4,1)S(1)} %fusion.172), kind=kOutput, calls=%fused_computation.60 | convolution fusion | flops 940376064 | bytes 15859776 | tf_op jit(solution)/shard_map/dot_general | solution.py:39
  417.7 5.4 all-to-all-start.4
  424.1 10.0 %all-to-all-done.4 = bf16[32,2,3584]{2,1,0:T(2,128)(2,1)S(1)} async-done(((bf16[32,2,3584]{2,1,0:T(2,128)(2,1)}), bf16[32,2,3584]{2,1,0:T(2,128)(2,1)S(1)}, u32[]{:S(2)}, u32[]{:S(2)}) %all-to-all-start.4) | async-done | bytes 458784 | tf_op jit(solution)/shard_map/all_to_all | solution.py:51
  446.0 40.4 %all-gather.18.cloned.1.call-done = bf16[256,3584]{1,0:T(8,128)(2,1)} async-done(((bf16[8,3584]{1,0:T(8,128)(2,1)}), bf16[256,3584]{1,0:T(8,128)(2,1)}) %all-gather.18.cloned.1.call-update) | async-done | bytes 1835024 | tf_op jit(solution)/shard_map/all_gather | solution.py:90
  494.0 8.0 %fusion.57 = bf16[64,3584]{1,0:T(8,128)(2,1)S(1)} fusion(bf16[1,1,1024,3584]{3,2,1,0:T(8,128)(2,1)} %param.12, bf16[1,1,3584,1024]{3,2,1,0:T(8,128)(2,1)} %param.11, f32[64,1024]{1,0:T(8,128)S(1)} %fusion.30, bf16[64,3584]{1,0:T(8,128)(2,1)S(1)} %gather_fusion.10, pred[64]{0:T(512)(128)(4,1)S(1)} %fusion.170), kind=kOutput, calls=%fused_computation.61 | convolution fusion | flops 940376064 | bytes 15859776 | tf_op jit(solution)/shard_map/dot_general | solution.py:39
  503.0 5.2 all-to-all-start.5
  509.2 10.0 %all-to-all-done.5 = bf16[32,2,3584]{2,1,0:T(2,128)(2,1)S(1)} async-done(((bf16[32,2,3584]{2,1,0:T(2,128)(2,1)}), bf16[32,2,3584]{2,1,0:T(2,128)(2,1)S(1)}, u32[]{:S(2)}, u32[]{:S(2)}) %all-to-all-start.5) | async-done | bytes 458784 | tf_op jit(solution)/shard_map/all_to_all | solution.py:51
  530.6 40.9 %all-gather.20.cloned.1.call-done = bf16[256,3584]{1,0:T(8,128)(2,1)} async-done(((bf16[8,3584]{1,0:T(8,128)(2,1)}), bf16[256,3584]{1,0:T(8,128)(2,1)}) %all-gather.20.cloned.1.call-update) | async-done | bytes 1835024 | tf_op jit(solution)/shard_map/all_gather | solution.py:90
  574.5 4.5 fusion.28
  579.0 8.0 %fusion.60 = bf16[64,3584]{1,0:T(8,128)(2,1)S(1)} fusion(bf16[1,1,1024,3584]{3,2,1,0:T(8,128)(2,1)} %param.12, bf16[1,1,3584,1024]{3,2,1,0:T(8,128)(2,1)} %param.11, f32[64,1024]{1,0:T(8,128)S(1)} %fusion.28, bf16[64,3584]{1,0:T(8,128)(2,1)S(1)} %gather_fusion.12, pred[64]{0:T(512)(128)(4,1)S(1)} %fusion.168), kind=kOutput, calls=%fused_computation.62 | convolution fusion | flops 940376064 | bytes 15859776 | tf_op jit(solution)/shard_map/dot_general | solution.py:39
  588.0 5.2 all-to-all-start.6
  594.2 10.0 %all-to-all-done.6 = bf16[32,2,3584]{2,1,0:T(2,128)(2,1)S(1)} async-done(((bf16[32,2,3584]{2,1,0:T(2,128)(2,1)}), bf16[32,2,3584]{2,1,0:T(2,128)(2,1)S(1)}, u32[]{:S(2)}, u32[]{:S(2)}) %all-to-all-start.6) | async-done | bytes 458784 | tf_op jit(solution)/shard_map/all_to_all | solution.py:51
  (337 shorter events, 147.7 us)
Async XLA Ops:
  6.5 76.3 %copy-start = (bf16[1,3584,32]{1,2,0:T(8,128)(2,1)S(1)}, bf16[1,3584,32]{1,2,0:T(8,128)(2,1)}, u32[]{:S(2)}) copy-start(bf16[1,3584,32]{1,2,0:T(8,128)(2,1)} %param.9) | copy-start | bytes 688132
  6.5 52.4 %copy-start.9 = (s32[1,4,8,8]{3,2,1,0:T(8,128)S(1)}, s32[1,4,8,8]{3,2,1,0:T(8,128)}, u32[]{:S(2)}) copy-start(s32[1,4,8,8]{3,2,1,0:T(8,128)} %param.13) | copy-start | bytes 3076
  6.5 54.5 %all-gather.8.cloned.1.call-start = ((), (), s32[]{:S(2)}) async-start(), calls=%async_computation.7 | async-start | bytes 1892352 | tf_op jit(solution)/shard_map/all_gather | solution.py:90
  77.6 16.1 %all-to-all-start = ((bf16[32,2,3584]{2,1,0:T(2,128)(2,1)}), bf16[32,2,3584]{2,1,0:T(2,128)(2,1)S(1)}, u32[]{:S(2)}, u32[]{:S(2)}) async-start(bf16[32,2,3584]{2,1,0:T(2,128)(2,1)} %reshape.520), calls=%async_computation | async-start | bytes 917504 | tf_op jit(solution)/shard_map/all_to_all | solution.py:51
  82.8 63.2 %all-gather.10.cloned.1.call-start = ((), (), s32[]{:S(2)}) async-start(), calls=%async_computation.8 | async-start | bytes 1892352 | tf_op jit(solution)/shard_map/all_gather | solution.py:90
  95.1 4.5 collective-permute-start
  97.7 6.1 collective-permute-start.1
  162.5 16.2 %all-to-all-start.1 = ((bf16[32,2,3584]{2,1,0:T(2,128)(2,1)}), bf16[32,2,3584]{2,1,0:T(2,128)(2,1)S(1)}, u32[]{:S(2)}, u32[]{:S(2)}) async-start(bf16[32,2,3584]{2,1,0:T(2,128)(2,1)} %reshape.524), calls=%async_computation.1 | async-start | bytes 917504 | tf_op jit(solution)/shard_map/all_to_all | solution.py:51
  167.7 63.3 %all-gather.12.cloned.1.call-start = ((), (), s32[]{:S(2)}) async-start(), calls=%async_computation.9 | async-start | bytes 1892352 | tf_op jit(solution)/shard_map/all_gather | solution.py:90
  180.0 4.6 collective-permute-start.2
  182.8 6.1 collective-permute-start.3
  246.7 28.8 %copy-start.23 = (s32[64]{0:T(128)S(1)}, s32[64]{0:T(128)}, u32[]{:S(2)}) copy-start(s32[64]{0:T(128)} %get-tuple-element.22) | copy-start | bytes 772
  247.6 16.2 %all-to-all-start.2 = ((bf16[32,2,3584]{2,1,0:T(2,128)(2,1)}), bf16[32,2,3584]{2,1,0:T(2,128)(2,1)S(1)}, u32[]{:S(2)}, u32[]{:S(2)}) async-start(bf16[32,2,3584]{2,1,0:T(2,128)(2,1)} %reshape.528), calls=%async_computation.2 | async-start | bytes 917504 | tf_op jit(solution)/shard_map/all_to_all | solution.py:51
  252.8 63.3 %all-gather.14.cloned.1.call-start = ((), (), s32[]{:S(2)}) async-start(), calls=%async_computation.10 | async-start | bytes 1892352 | tf_op jit(solution)/shard_map/all_gather | solution.py:90
  265.1 4.6 collective-permute-start.4
  267.9 6.1 collective-permute-start.5
  332.7 16.2 %all-to-all-start.3 = ((bf16[32,2,3584]{2,1,0:T(2,128)(2,1)}), bf16[32,2,3584]{2,1,0:T(2,128)(2,1)S(1)}, u32[]{:S(2)}, u32[]{:S(2)}) async-start(bf16[32,2,3584]{2,1,0:T(2,128)(2,1)} %reshape.532), calls=%async_computation.3 | async-start | bytes 917504 | tf_op jit(solution)/shard_map/all_to_all | solution.py:51
  337.8 63.3 %all-gather.16.cloned.1.call-start = ((), (), s32[]{:S(2)}) async-start(), calls=%async_computation.11 | async-start | bytes 1892352 | tf_op jit(solution)/shard_map/all_gather | solution.py:90
  350.2 4.6 collective-permute-start.6
  352.9 6.1 collective-permute-start.7
  416.8 28.8 %copy-start.15 = (s32[8,8]{1,0:T(8,128)S(1)}, s32[8,8]{1,0:T(8,128)}, u32[]{:S(2)}) copy-start(s32[8,8]{1,0:T(8,128)} %get-tuple-element.80) | copy-start | bytes 772
  416.8 28.8 %copy-start.14 = (s32[8,8]{1,0:T(8,128)S(1)}, s32[8,8]{1,0:T(8,128)}, u32[]{:S(2)}) copy-start(s32[8,8]{1,0:T(8,128)} %get-tuple-element.74) | copy-start | bytes 772
  416.8 29.0 %copy-start.21 = (s32[64]{0:T(128)S(1)}, s32[64]{0:T(128)}, u32[]{:S(2)}) copy-start(s32[64]{0:T(128)} %get-tuple-element.24) | copy-start | bytes 772
  417.7 16.4 %all-to-all-start.4 = ((bf16[32,2,3584]{2,1,0:T(2,128)(2,1)}), bf16[32,2,3584]{2,1,0:T(2,128)(2,1)S(1)}, u32[]{:S(2)}, u32[]{:S(2)}) async-start(bf16[32,2,3584]{2,1,0:T(2,128)(2,1)} %reshape.536), calls=%async_computation.4 | async-start | bytes 917504 | tf_op jit(solution)/shard_map/all_to_all | solution.py:51
  423.1 63.3 %all-gather.18.cloned.1.call-start = ((), (), s32[]{:S(2)}) async-start(), calls=%async_computation.12 | async-start | bytes 1892352 | tf_op jit(solution)/shard_map/all_gather | solution.py:90
  435.4 4.6 collective-permute-start.8
  438.2 6.1 collective-permute-start.9
  503.0 16.2 %all-to-all-start.5 = ((bf16[32,2,3584]{2,1,0:T(2,128)(2,1)}), bf16[32,2,3584]{2,1,0:T(2,128)(2,1)S(1)}, u32[]{:S(2)}, u32[]{:S(2)}) async-start(bf16[32,2,3584]{2,1,0:T(2,128)(2,1)} %reshape.540), calls=%async_computation.5 | async-start | bytes 917504 | tf_op jit(solution)/shard_map/all_to_all | solution.py:51
  508.2 63.3 %all-gather.20.cloned.1.call-start = ((), (), s32[]{:S(2)}) async-start(), calls=%async_computation.13 | async-start | bytes 1892352 | tf_op jit(solution)/shard_map/all_gather | solution.py:90
  520.5 4.6 collective-permute-start.10
  523.2 6.1 collective-permute-start.11
  588.0 16.2 %all-to-all-start.6 = ((bf16[32,2,3584]{2,1,0:T(2,128)(2,1)}), bf16[32,2,3584]{2,1,0:T(2,128)(2,1)S(1)}, u32[]{:S(2)}, u32[]{:S(2)}) async-start(bf16[32,2,3584]{2,1,0:T(2,128)(2,1)} %reshape.544), calls=%async_computation.6 | async-start | bytes 917504 | tf_op jit(solution)/shard_map/all_to_all | solution.py:51
  (20 other events, 377.4 us)
Sparse Core Ops, SparseCore 0:
  10.0 45.7 all-gather.7
  104.8 41.1 all-gather.9
  189.9 41.1 all-gather.11
  274.9 41.1 all-gather.13
  360.0 41.1 all-gather.15
  445.3 41.1 all-gather.17
  530.3 41.1 all-gather.19
where the time goes:
time: 625 us; the launch traced here: 613 us
  waiting for transfers between devices  342 us (55%)
  matrix products  94.3 us (15%)
  starting transfers between devices  61.5 us (10%)
  local copies, waits for them, and re-layouts  48.9 us (8%)
  blocking collectives  26.2 us (4%)
  other arithmetic  25.6 us (4%)
  between operations  15.2 us (2%)
    all_gather x7, waiting for transfers between devices, per_device(): everyone = lax.all_gather(normed, 'expert', axis=0, tiled=True)  244 us
    all_to_all x7, waiting for transfers between devices, send_back(): lax.all_to_all(produced, 'expert', split_axis=0, concat_axis=0, tiled=True)  69.7 us
    dot_general x7, matrix products, expert_mlp(): jnp.dot(hidden, down_weight, preferred_element_type=jnp.float32)  56.3 us
    all_to_all x7, starting transfers between devices, send_back(): lax.all_to_all(produced, 'expert', split_axis=0, concat_axis=0, tiled=True)  36.3 us
    dot_general x7, matrix products, expert_mlp(): gate_part = jnp.dot(inputs, gate_weight, preferred_element_type=jnp.float32)  31.7 us
    ppermute x12, waiting for transfers between devices, passed_along(): return lax.ppermute(block, axis, route)  28 us
    all_gather x1, blocking collectives, per_device(): every_ids = lax.all_gather(expert_ids, 'expert', axis=2, tiled=True)  26.2 us
    ppermute x12, starting transfers between devices, passed_along(): return lax.ppermute(block, axis, route)  24.8 us
  transfers between devices with their start and end apart: 26, of which 25 were waited for; matrix products, arithmetic and copies ran while one was open for 6% of the time, Pallas kernels for 0%

commit v1 on v0

v1 whole, which is shorter than its diff:
```python
import functools

import jax
import jax.numpy as jnp
from jax import lax
from jax.experimental import pallas as pl
from jax.experimental.pallas import tpu as pltpu
from jax.sharding import PartitionSpec as P

MESH = pl.DeviceIdType.MESH
BF16 = jnp.bfloat16
F32 = jnp.float32

epsilon = 1e-06
routed_scale = 2.5
capacity = 2
lane = 128
slot_rows = 32
message_rows = capacity * slot_rows


def dot(a, b):
    return jnp.dot(a, b, preferred_element_type=F32)


def iota(shape, dim):
    return lax.broadcasted_iota(jnp.int32, shape, dim)


def ones_where(mask, dtype=BF16):
    return jnp.where(mask, 1.0, 0.0).astype(dtype)


def schedule(micros):
    order = [(0, 0)]
    for m in range(micros):
        if m + 1 < micros:
            order.append((0, m + 1))
        order.append((1, m))
        if m >= 1:
            order.append((2, m - 1))
    order.append((2, micros - 1))
    return order


def kernel(
    grid_z, grid_x, sections, chunks, tokens, gain, router, w_gate, w_up, w_down, ids, result,
    gate_v, up_v, down_v, hidden, finished, staged, outgoing,
    place, pick, factors, stacked, dispatched, arrived, produced, returned,
    rows_in, inner, columns, select, select_t, spread, mask_j,
    gate_sem, up_sem, down_sem, hidden_sem, hidden_send, finished_sem,
    dispatch_send, arrive_sem, produce_send, return_sem, local_sem,
):
    section = lax.axis_index("section")
    me = lax.axis_index("expert")
    experts = grid_z * grid_x * 2
    micros = sections
    rows = 8
    width = chunks * lane
    half = width // 2
    inner_width = gate_v.shape[1]
    core, x, z = lax.rem(me, 2), lax.rem(me // 2, grid_x), me // (2 * grid_x)

    def distance(step, size):
        return min(step, size - step)

    offsets = [(dz, dx, dc) for dz in range(grid_z) for dx in range(grid_x) for dc in range(2)]
    offsets.sort(key=lambda o: -(10 * (distance(o[0], grid_z) + distance(o[1], grid_x)) + o[2]))
    partners = []
    for dz, dx, dc in offsets[:-1]:
        partners.append(
            lax.rem(z + dz, grid_z) * (2 * grid_x) + lax.rem(x + dx, grid_x) * 2 + lax.rem(core + dc, 2)
        )

    copy_gate = pltpu.make_async_copy(w_gate.at[0, 0], gate_v, gate_sem)
    copy_up = pltpu.make_async_copy(w_up.at[0, 0], up_v, up_sem)
    copy_down = pltpu.make_async_copy(w_down.at[0, 0], down_v, down_sem)
    copy_gate.start()
    copy_up.start()
    copy_down.start()

    barrier = pltpu.get_barrier_semaphore()
    for partner in partners:
        pl.semaphore_signal(barrier, inc=1, device_id={"expert": partner}, device_id_type=MESH)
    for step in range(1, sections):
        pl.semaphore_signal(
            barrier, inc=1, device_id={"section": lax.rem(section + step, sections)}, device_id_type=MESH
        )

    used = chunks * rows
    shape = (used, 4 * message_rows)
    r, c = iota(shape, 0), iota(shape, 1)
    select[...] = ones_where(c == ((r % 8) // 2) * message_rows + (r % 2) * slot_rows + r // 8)
    shape = (4 * message_rows, 256)
    r, c = iota(shape, 0), iota(shape, 1)
    select_t[...] = ones_where(
        (c < used) & (r == ((c % 8) // 2) * message_rows + (c % 2) * slot_rows + c // 8)
    )
    shape = (experts, experts * message_rows)
    r, c = iota(shape, 0), iota(shape, 1)
    for p in range(capacity):
        spread[p] = ones_where((c // message_rows == r) & ((c % message_rows) // slot_rows == p))
    shape = (chunks * 16, lane)
    r, c = iota(shape, 0), iota(shape, 1)
    mask_j[...] = ones_where(c % slot_rows == r // 16)
    for m in range(micros):
        stacked[m, used:, :] = jnp.zeros((256 - used, lane), BF16)
    for g in range(experts // 4):
        columns[g, used:, :] = jnp.zeros((256 - used, lane), BF16)

    shape = (slot_rows, 256)
    r, c = iota(shape, 0), iota(shape, 1)
    diagonal = jnp.where((c // rows == r) & (r < chunks), 1.0, 0.0).astype(F32)
    repeat = jnp.where(iota((rows, 256), 1) % rows == iota((rows, 256), 0), 1.0, 0.0).astype(F32)
    token_of = iota((rows, experts), 0)
    expert_of = iota((rows, experts), 1)

    def plan(m, _):
        choices = ids[0, m]
        hit = jnp.zeros((rows, experts), F32)
        for k in range(choices.shape[1]):
            hit = hit + jnp.where(choices[:, k : k + 1] == expert_of, 1.0, 0.0)
        before = jnp.zeros((rows, experts), F32)
        for t in range(rows - 1):
            before = before + jnp.where(token_of > t, 1.0, 0.0) * hit[t : t + 1, :]
        for p in range(capacity):
            taken = jnp.where(before == float(p), hit, 0.0)
            pick[m, p] = taken
            lanes = lax.dot_general(
                taken, repeat, (((0,), (0,)), ((), ())), preferred_element_type=F32
            )
            for e in range(experts):
                place[m, e * message_rows + p * slot_rows : e * message_rows + (p + 1) * slot_rows, :] = (
                    diagonal * lanes[e : e + 1, :]
                ).astype(BF16)
        return 0

    lax.fori_loop(0, micros, plan, 0)

    held = tokens[0].astype(F32)
    staged[...] = jnp.concatenate([held[:, :half], held[:, half:]], axis=0).astype(BF16)
    pl.semaphore_wait(barrier, len(partners) + sections - 1)

    first_copy = pltpu.make_async_remote_copy(
        src_ref=staged, dst_ref=hidden.at[section], send_sem=local_sem, recv_sem=hidden_sem.at[section],
        device_id={"section": 0}, device_id_type=MESH,
    )

    @pl.when(section == 0)
    def _():
        hidden[0] = staged[...]

    @pl.when(section != 0)
    def _():
        first_copy.start()

    def load_hidden(m):
        packed = hidden[m].astype(F32)
        return jnp.concatenate([packed[:rows], packed[rows:]], axis=1)

    def dispatch(m):
        @pl.when((section != 0) | (m != 0))
        def _():
            pltpu.make_async_copy(hidden.at[m], hidden.at[m], hidden_sem.at[m]).wait()

        values = load_hidden(m)
        inverse_rms = lax.rsqrt(jnp.mean(values * values, axis=-1, keepdims=True) + epsilon)
        normed = values * inverse_rms * gain[...].astype(F32)
        stacked[m, :used, :] = jnp.concatenate(
            [normed[:, j * lane : (j + 1) * lane] for j in range(chunks)], axis=0
        ).astype(BF16)
        dispatched[m] = dot(place[m], stacked[m]).astype(BF16)
        here = pl.multiple_of(me * message_rows, message_rows)
        for partner in partners:
            there = pl.multiple_of(partner * message_rows, message_rows)
            pltpu.make_async_remote_copy(
                src_ref=dispatched.at[m, pl.ds(there, message_rows)],
                dst_ref=arrived.at[m, pl.ds(here, message_rows)],
                send_sem=dispatch_send.at[m], recv_sem=arrive_sem.at[m],
                device_id={"expert": partner}, device_id_type=MESH,
            ).start()
        pltpu.make_async_copy(
            dispatched.at[m, pl.ds(here, message_rows)],
            arrived.at[m, pl.ds(here, message_rows)],
            arrive_sem.at[m],
        ).start()

        twice = jnp.concatenate([normed, normed], axis=0).astype(BF16)
        scores = jax.nn.sigmoid(dot(twice, router[0])[:rows])
        kept = [pick[m, p] for p in range(capacity)]
        chosen = jnp.zeros((rows, experts), F32)
        for k in range(ids.shape[3]):
            chosen = chosen + jnp.where(ids[0, m][:, k : k + 1] == expert_of, scores, 0.0)
        weights = routed_scale * scores / jnp.sum(chosen, axis=-1, keepdims=True)
        wide = None
        for p in range(capacity):
            factor = weights * kept[p]
            high = factor.astype(BF16).astype(F32)
            both = jnp.concatenate([high, factor - high], axis=0).astype(BF16)
            part = dot(both, spread[p])
            wide = part if wide is None else wide + part
        wide = wide.astype(BF16)
        for j in range(chunks):
            mask = mask_j[j * 16 : (j + 1) * 16, :]
            factors[m, j * 16 : (j + 1) * 16, :] = wide * jnp.concatenate(
                [mask] * (experts * message_rows // lane), axis=1
            )

    def run_experts(m):
        pltpu.make_async_copy(arrived.at[m], arrived.at[m], arrive_sem.at[m]).wait()
        group = 4 * message_rows
        for pair in range(experts // 8):
            first = arrived[m, (2 * pair) * group : (2 * pair + 1) * group, :]
            second = arrived[m, (2 * pair + 1) * group : (2 * pair + 2) * group, :]
            sorted_rows = dot(select[...], jnp.concatenate([first, second], axis=1))
            for j in range(chunks):
                tile = sorted_rows[j * 8 : (j + 1) * 8, :]
                rows_in[pair * 16 : (pair + 1) * 16, j * lane : (j + 1) * lane] = jnp.concatenate(
                    [tile[:, :lane], tile[:, lane:]], axis=0
                ).astype(BF16)

        @pl.when(m == 0)
        def _():
            copy_gate.wait()
            copy_up.wait()

        for n in range(inner_width // 256):
            cols = slice(n * 256, (n + 1) * 256)
            gate_part = dot(rows_in[...], gate_v[:, cols])
            up_part = dot(rows_in[...], up_v[:, cols])
            inner[:, cols] = (gate_part / (1.0 + jnp.exp(-gate_part)) * up_part).astype(BF16)

        @pl.when(m == 0)
        def _():
            copy_down.wait()

        step = 4
        for n in range(chunks // step):
            out = dot(inner[...], down_v[:, n * step * lane : (n + 1) * step * lane])
            for g in range(experts // 4):
                columns[g, n * step * 8 : (n + 1) * step * 8, :] = jnp.concatenate(
                    [out[g * 8 : (g + 1) * 8, j * lane : (j + 1) * lane] for j in range(step)], axis=0
                ).astype(BF16)
        for pair in range(experts // 8):
            both = jnp.concatenate([columns[2 * pair], columns[2 * pair + 1]], axis=1)
            back = dot(select_t[...], both).astype(BF16)
            produced[m, (2 * pair) * group : (2 * pair + 1) * group, :] = back[:, :lane]
            produced[m, (2 * pair + 1) * group : (2 * pair + 2) * group, :] = back[:, lane:]
        here = pl.multiple_of(me * message_rows, message_rows)
        for partner in partners:
            there = pl.multiple_of(partner * message_rows, message_rows)
            pltpu.make_async_remote_copy(
                src_ref=produced.at[m, pl.ds(there, message_rows)],
                dst_ref=returned.at[m, pl.ds(here, message_rows)],
                send_sem=produce_send.at[m], recv_sem=return_sem.at[m],
                device_id={"expert": partner}, device_id_type=MESH,
            ).start()
        pltpu.make_async_copy(
            produced.at[m, pl.ds(here, message_rows)],
            returned.at[m, pl.ds(here, message_rows)],
            return_sem.at[m],
        ).start()

    def combine(m):
        pltpu.make_async_copy(returned.at[m], returned.at[m], return_sem.at[m]).wait()
        branch = dot(factors[m], returned[m])
        values = load_hidden(m)
        fresh = []
        for j in range(chunks):
            part = branch[j * 16 : j * 16 + 8, :] + branch[j * 16 + 8 : j * 16 + 16, :]
            fresh.append(values[:, j * lane : (j + 1) * lane] + part)
        split = chunks // 2
        outgoing[m] = jnp.concatenate(
            [jnp.concatenate(fresh[:split], axis=1), jnp.concatenate(fresh[split:], axis=1)], axis=0
        ).astype(BF16)

        @pl.when(section < sections - 1)
        def _():
            pltpu.make_async_remote_copy(
                src_ref=outgoing.at[m], dst_ref=hidden.at[m],
                send_sem=hidden_send.at[m], recv_sem=hidden_sem.at[m],
                device_id={"section": lax.rem(section + 1, sections)}, device_id_type=MESH,
            ).start()

        @pl.when((section == sections - 1) & (m < micros - 1))
        def _():
            pltpu.make_async_remote_copy(
                src_ref=outgoing.at[m], dst_ref=finished,
                send_sem=hidden_send.at[m], recv_sem=finished_sem,
                device_id={"section": lax.rem(m, sections)}, device_id_type=MESH,
            ).start()

        @pl.when((section == sections - 1) & (m == micros - 1))
        def _():
            finished[...] = outgoing[m]

    order = schedule(micros)

    def stage(i, _):
        kind, m = jnp.int32(order[0][0]), jnp.int32(order[0][1])
        for index, (k, micro) in enumerate(order):
            kind = jnp.where(i == index, k, kind)
            m = jnp.where(i == index, micro, m)

        @pl.when(kind == 0)
        def _():
            dispatch(m)

        @pl.when(kind == 1)
        def _():
            run_experts(m)

        @pl.when(kind == 2)
        def _():
            combine(m)

        return 0

    lax.fori_loop(0, len(order), stage, 0)

    @pl.when(section < sections - 1)
    def _():
        pltpu.make_async_copy(finished, finished, finished_sem).wait()

    packed = finished[...].astype(F32)
    result[0] = jnp.concatenate([packed[:rows], packed[rows:]], axis=1).astype(BF16)

    @pl.when(section != 0)
    def _():
        first_copy.wait_send()

    def drain(m, _):
        sent = len(partners) * message_rows
        for source, semaphore in ((dispatched, dispatch_send), (produced, produce_send)):
            view = source.at[m, pl.ds(0, sent)]
            pltpu.make_async_copy(view, view, semaphore.at[m]).wait()

        @pl.when((section < sections - 1) | (m < micros - 1))
        def _():
            pltpu.make_async_copy(outgoing.at[m], outgoing.at[m], hidden_send.at[m]).wait()

        return 0

    lax.fori_loop(0, micros, drain, 0)


def solution(mesh):
    sections = mesh.shape["section"]
    experts = mesh.shape["expert"]
    grid_z = grid_x = int(round((experts // 2) ** 0.5))

    def per_device(tokens, norm_gain, router, w_gate, w_up, w_down, expert_ids):
        rows, width = tokens.shape[1:]
        inner_width = w_gate.shape[3]
        chunks = width // lane
        micros = expert_ids.shape[1]
        used = chunks * rows
        slots = experts * capacity
        messages = experts * message_rows
        vmem = pl.BlockSpec(memory_space=pltpu.VMEM)
        anywhere = pl.BlockSpec(memory_space=pl.ANY)
        dma = pltpu.SemaphoreType.DMA
        packed = (2 * rows, width // 2)
        return pl.pallas_call(
            functools.partial(kernel, grid_z, grid_x, sections, chunks),
            out_shape=jax.ShapeDtypeStruct(tokens.shape, BF16),
            in_specs=[vmem, vmem, vmem, anywhere, anywhere, anywhere, vmem],
            out_specs=vmem,
            scratch_shapes=[
                pltpu.VMEM((width, inner_width), BF16),
                pltpu.VMEM((width, inner_width), BF16),
                pltpu.VMEM((inner_width, width), BF16),
                pltpu.VMEM((micros,) + packed, BF16),
                pltpu.VMEM(packed, BF16),
                pltpu.VMEM(packed, BF16),
                pltpu.VMEM((micros,) + packed, BF16),
                pltpu.VMEM((micros, messages, 256), BF16),
                pltpu.VMEM((micros, capacity, rows, experts), F32),
                pltpu.VMEM((micros, chunks * 16, messages), BF16),
                pltpu.VMEM((micros, 256, lane), BF16),
                pltpu.VMEM((micros, messages, lane), BF16),
                pltpu.VMEM((micros, messages, lane), BF16),
                pltpu.VMEM((micros, messages, lane), BF16),
                pltpu.VMEM((micros, messages, lane), BF16),
                pltpu.VMEM((slots, width), BF16),
                pltpu.VMEM((slots, inner_width), BF16),
                pltpu.VMEM((experts // 4, 256, lane), BF16),
                pltpu.VMEM((used, 4 * message_rows), BF16),
                pltpu.VMEM((4 * message_rows, 256), BF16),
                pltpu.VMEM((capacity, experts, messages), BF16),
                pltpu.VMEM((chunks * 16, lane), BF16),
                dma, dma, dma,
                dma((micros,)), dma((micros,)), dma,
                dma((micros,)), dma((micros,)), dma((micros,)), dma((micros,)), dma,
            ],
            compiler_params=pltpu.CompilerParams(
                collective_id=0, has_side_effects=True, vmem_limit_bytes=58 * 2**20
            ),
            name="expert_layers",
        )(tokens, norm_gain, router, w_gate, w_up, w_down, expert_ids)

    placed = (
        P("section", "expert", None),
        P("section", None),
        P("section", None, None),
        P("section", "expert", None, None),
        P("section", "expert", None, None),
        P("section", "expert", None, None),
        P("section", None, "expert", None),
    )
    return jax.shard_map(
        per_device,
        mesh=mesh,
        in_specs=placed,
        out_specs=P("section", "expert", None),
        check_vma=False,
    )
```

time: 625 us -> 163 us (0.26); the launches traced: 613 us -> 163 us
  waiting for transfers between devices: 342 us -> 0 us
  Pallas kernels: 0 us -> 159 us
  matrix products: 94.3 us -> 0 us
  starting transfers between devices: 61.5 us -> 0 us
  local copies, waits for them, and re-layouts: 48.9 us -> 3.62 us
  blocking collectives: 26.2 us -> 0 us
  other arithmetic: 25.6 us -> 0 us
  between operations: 15.2 us -> 0.01 us
    all_gather x7 -> x0, waiting for transfers between devices: 244 us -> none  [per_device(): everyone = lax.all_gather(normed, 'expert', axis=0, tiled=True)]
    pallas_call x0 -> x1, Pallas kernels: none -> 159 us  [per_device(): pl.pallas_call(functools.partial(kernel, grid_z, grid_x, sections, chunks...]
    dot_general x28 -> x0, matrix products: 94.3 us -> none  [the longest x7 56.3 us: expert_mlp(): jnp.dot(hidden, down_weight, preferred_element_type=jnp.float32)]
    all_to_all x7 -> x0, waiting for transfers between devices: 69.7 us -> none  [send_back(): lax.all_to_all(produced, 'expert', split_axis=0, concat_axis=0, tiled=True)]
    all_to_all x7 -> x0, starting transfers between devices: 36.3 us -> none  [send_back(): lax.all_to_all(produced, 'expert', split_axis=0, concat_axis=0, tiled=True)]
    ppermute x12 -> x0, waiting for transfers between devices: 28 us -> none  [passed_along(): return lax.ppermute(block, axis, route)]
    gather x14 -> x0, local copies, waits for them, and re-layouts: 26.9 us -> none  [the longest x7 21.1 us: fill_slots(): normed[source]]
    all_gather x1 -> x0, blocking collectives: 26.2 us -> none  [per_device(): every_ids = lax.all_gather(expert_ids, 'expert', axis=2, tiled=True)]
  transfers between devices with their start and end apart: 26 -> 0, of which waited for: 25 -> 0; matrix products, arithmetic and copies ran while one was open for 6% -> 0% of each run, Pallas kernels for 0% -> 0%
where the time goes in v1:
time: 163 us
  Pallas kernels  159 us (98%)
  local copies, waits for them, and re-layouts  3.62 us (2%)
    pallas_call x1, Pallas kernels, per_device(): pl.pallas_call(functools.partial(kernel, grid_z, grid_x, sections, chunks...  159 us
    unnamed x2, local copies, waits for them, and re-layouts  3.62 us

profile of v1, /device:TPU:24, one launch (start us, length us, event | category | flops | bytes accessed | tf_op | source)
XLA Modules:
  0.0 162.8 jit_solution(12747064228845977847)
XLA Ops:
  0.0 2.2 %copy.8.router = bf16[1,3584,32]{2,1,0:T(8,128)(2,1)} copy(bf16[1,3584,32]{1,2,0:T(8,128)(2,1)} %param.9) | data formatting | bytes 458752 | tf_op args[2]
  2.2 159.2 %expert_layers.1 = bf16[1,8,3584]{2,1,0:T(8,128)(2,1)} custom-call(bf16[1,8,3584]{2,1,0:T(8,128)(2,1)} %tokens.1, bf16[1,3584]{1,0:T(2,128)(2,1)} %gain.1, bf16[1,3584,32]{2,1,0:T(8,128)(2,1)} %copy.8.router, bf16[1,1,3584,1024]{3,2,1,0:T(8,128)(2,1)} %w_gate.1, bf16[1,1,3584,1024]{3,2,1,0:T(8,128)(2,1)} %w_up.1, bf16[1,1,1024,3584]{3,2,1,0:T(8,128)(2,1)} %w_down.1, ...), custom_call_target="tpu_custom_call" | custom-call | tf_op jit(solution)/shard_map/expert_layers/pallas_call | solution.py:364
  161.4 1.4 copy.10

commit v2 on v1

--- a/solution.py
+++ b/solution.py
@@ -15,8 +15,7 @@
 routed_scale = 2.5
 capacity = 2
 lane = 128
-slot_rows = 32
-message_rows = capacity * slot_rows
+message_rows = 64
 
 
 def dot(a, b):
@@ -32,15 +31,13 @@
 
 
 def schedule(micros):
-    order = [(0, 0)]
-    for m in range(micros):
-        if m + 1 < micros:
-            order.append((0, m + 1))
-        order.append((1, m))
-        if m >= 1:
-            order.append((2, m - 1))
-    order.append((2, micros - 1))
-    return order
+    order = []
+    for m in range(0, micros, 2):
+        if m:
+            order += [(2, m - 2), (0, m), (2, m - 1), (0, m + 1), (1, m), (1, m + 1)]
+        else:
+            order += [(0, 0), (0, 1), (1, 0), (1, 1)]
+    return order + [(2, micros - 2), (2, micros - 1)]
 
 
 def kernel(
@@ -79,6 +76,10 @@
     copy_up.start()
     copy_down.start()
 
+    for room in (arrived, returned):
+        for m in range(micros):
+            room[m, :, message_rows - 16 :, :] = jnp.zeros((experts, 16, lane), BF16)
+
     barrier = pltpu.get_barrier_semaphore()
     for partner in partners:
         pl.semaphore_signal(barrier, inc=1, device_id={"expert": partner}, device_id_type=MESH)
@@ -88,34 +89,21 @@
         )
 
     used = chunks * rows
-    shape = (used, 4 * message_rows)
-    r, c = iota(shape, 0), iota(shape, 1)
-    select[...] = ones_where(c == ((r % 8) // 2) * message_rows + (r % 2) * slot_rows + r // 8)
-    shape = (4 * message_rows, 256)
-    r, c = iota(shape, 0), iota(shape, 1)
-    select_t[...] = ones_where(
-        (c < used) & (r == ((c % 8) // 2) * message_rows + (c % 2) * slot_rows + c // 8)
-    )
-    shape = (experts, experts * message_rows)
-    r, c = iota(shape, 0), iota(shape, 1)
-    for p in range(capacity):
-        spread[p] = ones_where((c // message_rows == r) & ((c % message_rows) // slot_rows == p))
-    shape = (chunks * 16, lane)
-    r, c = iota(shape, 0), iota(shape, 1)
-    mask_j[...] = ones_where(c % slot_rows == r // 16)
+    sent = chunks * capacity
     for m in range(micros):
         stacked[m, used:, :] = jnp.zeros((256 - used, lane), BF16)
-    for g in range(experts // 4):
-        columns[g, used:, :] = jnp.zeros((256 - used, lane), BF16)
-
-    shape = (slot_rows, 256)
+
+    shape = (message_rows, 256)
     r, c = iota(shape, 0), iota(shape, 1)
-    diagonal = jnp.where((c // rows == r) & (r < chunks), 1.0, 0.0).astype(F32)
+    diagonal = [
+        jnp.where((c // rows == r // capacity) & (r % capacity == p) & (r < sent), 1.0, 0.0).astype(F32)
+        for p in range(capacity)
+    ]
     repeat = jnp.where(iota((rows, 256), 1) % rows == iota((rows, 256), 0), 1.0, 0.0).astype(F32)
     token_of = iota((rows, experts), 0)
     expert_of = iota((rows, experts), 1)
 
-    def plan(m, _):
+    def plan(m, _=0):
         choices = ids[0, m]
         hit = jnp.zeros((rows, experts), F32)
         for k in range(choices.shape[1]):
@@ -123,70 +111,55 @@
         before = jnp.zeros((rows, experts), F32)
         for t in range(rows - 1):
             before = before + jnp.where(token_of > t, 1.0, 0.0) * hit[t : t + 1, :]
+        lanes = []
         for p in range(capacity):
             taken = jnp.where(before == float(p), hit, 0.0)
             pick[m, p] = taken
-            lanes = lax.dot_general(
-                taken, repeat, (((0,), (0,)), ((), ())), preferred_element_type=F32
+            lanes.append(
+                lax.dot_general(taken, repeat, (((0,), (0,)), ((), ())), preferred_element_type=F32)
             )
-            for e in range(experts):
-                place[m, e * message_rows + p * slot_rows : e * message_rows + (p + 1) * slot_rows, :] = (
-                    diagonal * lanes[e : e + 1, :]
-                ).astype(BF16)
+        for e in range(experts):
+            block = diagonal[0] * lanes[0][e : e + 1, :] + diagonal[1] * lanes[1][e : e + 1, :]
+            place[m, e * message_rows : (e + 1) * message_rows, :] = block.astype(BF16)
         return 0
-
-    lax.fori_loop(0, micros, plan, 0)
-
-    held = tokens[0].astype(F32)
-    staged[...] = jnp.concatenate([held[:, :half], held[:, half:]], axis=0).astype(BF16)
-    pl.semaphore_wait(barrier, len(partners) + sections - 1)
-
-    first_copy = pltpu.make_async_remote_copy(
-        src_ref=staged, dst_ref=hidden.at[section], send_sem=local_sem, recv_sem=hidden_sem.at[section],
-        device_id={"section": 0}, device_id_type=MESH,
-    )
-
-    @pl.when(section == 0)
-    def _():
-        hidden[0] = staged[...]
-
-    @pl.when(section != 0)
-    def _():
-        first_copy.start()
 
     def load_hidden(m):
         packed = hidden[m].astype(F32)
         return jnp.concatenate([packed[:rows], packed[rows:]], axis=1)
 
-    def dispatch(m):
-        @pl.when((section != 0) | (m != 0))
-        def _():
-            pltpu.make_async_copy(hidden.at[m], hidden.at[m], hidden_sem.at[m]).wait()
-
+    def normalize(m):
         values = load_hidden(m)
         inverse_rms = lax.rsqrt(jnp.mean(values * values, axis=-1, keepdims=True) + epsilon)
-        normed = values * inverse_rms * gain[...].astype(F32)
+        return values * inverse_rms * gain[...].astype(F32)
+
+    def fill_slots(m):
+        normed = normalize(m)
         stacked[m, :used, :] = jnp.concatenate(
             [normed[:, j * lane : (j + 1) * lane] for j in range(chunks)], axis=0
         ).astype(BF16)
-        dispatched[m] = dot(place[m], stacked[m]).astype(BF16)
-        here = pl.multiple_of(me * message_rows, message_rows)
+        dispatched[m] = dot(place[m], stacked[m]).astype(BF16).reshape(experts, message_rows, lane)
+
+    def send_slots(m):
         for partner in partners:
-            there = pl.multiple_of(partner * message_rows, message_rows)
             pltpu.make_async_remote_copy(
-                src_ref=dispatched.at[m, pl.ds(there, message_rows)],
-                dst_ref=arrived.at[m, pl.ds(here, message_rows)],
+                src_ref=dispatched.at[m, partner, pl.ds(0, sent)],
+                dst_ref=arrived.at[m, me, pl.ds(0, sent)],
                 send_sem=dispatch_send.at[m], recv_sem=arrive_sem.at[m],
                 device_id={"expert": partner}, device_id_type=MESH,
             ).start()
         pltpu.make_async_copy(
-            dispatched.at[m, pl.ds(here, message_rows)],
-            arrived.at[m, pl.ds(here, message_rows)],
+            dispatched.at[m, me, pl.ds(0, sent)],
+            arrived.at[m, me, pl.ds(0, sent)],
             arrive_sem.at[m],
         ).start()
 
+    def spread_factors(m):
+        normed = normalize(m)
         twice = jnp.concatenate([normed, normed], axis=0).astype(BF16)
-        scores = jax.nn.sigmoid(dot(twice, router[0])[:rows])
+        logits = lax.dot_general(
+            twice, router[0], (((1,), (1,)), ((), ())), preferred_element_type=F32
+        )
+        scores = jax.nn.sigmoid(logits[:rows])
         kept = [pick[m, p] for p in range(capacity)]
         chosen = jnp.zeros((rows, experts), F32)
         for k in range(ids.shape[3]):
@@ -206,12 +179,22 @@
                 [mask] * (experts * message_rows // lane), axis=1
             )
 
+    def dispatch(m):
+        @pl.when((section != 0) | (m != 0))
+        def _():
+            pltpu.make_async_copy(hidden.at[m], hidden.at[m], hidden_sem.at[m]).wait()
+            fill_slots(m)
+            send_slots(m)
+
+        spread_factors(m)
+
     def run_experts(m):
-        pltpu.make_async_copy(arrived.at[m], arrived.at[m], arrive_sem.at[m]).wait()
+        view = arrived.at[m, :, pl.ds(0, sent)]
+        pltpu.make_async_copy(view, view, arrive_sem.at[m]).wait()
         group = 4 * message_rows
         for pair in range(experts // 8):
-            first = arrived[m, (2 * pair) * group : (2 * pair + 1) * group, :]
-            second = arrived[m, (2 * pair + 1) * group : (2 * pair + 2) * group, :]
+            first = arrived[m, 8 * pair : 8 * pair + 4].reshape(group, lane)
+            second = arrived[m, 8 * pair + 4 : 8 * pair + 8].reshape(group, lane)
             sorted_rows = dot(select[...], jnp.concatenate([first, second], axis=1))
             for j in range(chunks):
                 tile = sorted_rows[j * 8 : (j + 1) * 8, :]
@@ -244,26 +227,25 @@
         for pair in range(experts // 8):
             both = jnp.concatenate([columns[2 * pair], columns[2 * pair + 1]], axis=1)
             back = dot(select_t[...], both).astype(BF16)
-            produced[m, (2 * pair) * group : (2 * pair + 1) * group, :] = back[:, :lane]
-            produced[m, (2 * pair + 1) * group : (2 * pair + 2) * group, :] = back[:, lane:]
-        here = pl.multiple_of(me * message_rows, message_rows)
+            produced[m, 8 * pair : 8 * pair + 4] = back[:, :lane].reshape(4, message_rows, lane)
+            produced[m, 8 * pair + 4 : 8 * pair + 8] = back[:, lane:].reshape(4, message_rows, lane)
         for partner in partners:
-            there = pl.multiple_of(partner * message_rows, message_rows)
             pltpu.make_async_remote_copy(
-                src_ref=produced.at[m, pl.ds(there, message_rows)],
-                dst_ref=returned.at[m, pl.ds(here, message_rows)],
+                src_ref=produced.at[m, partner, pl.ds(0, sent)],
+                dst_ref=returned.at[m, me, pl.ds(0, sent)],
                 send_sem=produce_send.at[m], recv_sem=return_sem.at[m],
                 device_id={"expert": partner}, device_id_type=MESH,
             ).start()
         pltpu.make_async_copy(
-            produced.at[m, pl.ds(here, message_rows)],
-            returned.at[m, pl.ds(here, message_rows)],
+            produced.at[m, me, pl.ds(0, sent)],
+            returned.at[m, me, pl.ds(0, sent)],
             return_sem.at[m],
         ).start()
 
     def combine(m):
-        pltpu.make_async_copy(returned.at[m], returned.at[m], return_sem.at[m]).wait()
-        branch = dot(factors[m], returned[m])
+        view = returned.at[m, :, pl.ds(0, sent)]
+        pltpu.make_async_copy(view, view, return_sem.at[m]).wait()
+        branch = dot(factors[m], returned[m].reshape(experts * message_rows, lane))
         values = load_hidden(m)
         fresh = []
         for j in range(chunks):
@@ -294,6 +276,50 @@
         def _():
             finished[...] = outgoing[m]
 
+    held = tokens[0].astype(F32)
+    staged[...] = jnp.concatenate([held[:, :half], held[:, half:]], axis=0).astype(BF16)
+    plan(0)
+
+    @pl.when(section == 0)
+    def _():
+        hidden[0] = staged[...]
+        fill_slots(0)
+
+    pl.semaphore_wait(barrier, len(partners) + sections - 1)
+
+    first_copy = pltpu.make_async_remote_copy(
+        src_ref=staged, dst_ref=hidden.at[section], send_sem=local_sem, recv_sem=hidden_sem.at[section],
+        device_id={"section": 0}, device_id_type=MESH,
+    )
+
+    @pl.when(section == 0)
+    def _():
+        send_slots(0)
+
+    @pl.when(section != 0)
+    def _():
+        first_copy.start()
+
+    shape = (used, 4 * message_rows)
+    r, c = iota(shape, 0), iota(shape, 1)
+    select[...] = ones_where(c == ((r % 8) // 2) * message_rows + (r // 8) * 2 + r % 2)
+    shape = (4 * message_rows, 256)
+    r, c = iota(shape, 0), iota(shape, 1)
+    select_t[...] = ones_where(
+        (c < used) & (r == ((c % 8) // 2) * message_rows + (c // 8) * 2 + c % 2)
+    )
+    shape = (experts, experts * message_rows)
+    r, c = iota(shape, 0), iota(shape, 1)
+    for p in range(capacity):
+        spread[p] = ones_where((c // message_rows == r) & (c % capacity == p))
+    shape = (chunks * 16, lane)
+    r, c = iota(shape, 0), iota(shape, 1)
+    mask_j[...] = ones_where((c % message_rows) // capacity == r // 16)
+    for g in range(experts // 4):
+        columns[g, used:, :] = jnp.zeros((256 - used, lane), BF16)
+
+    lax.fori_loop(1, micros, plan, 0)
+
     order = schedule(micros)
 
     def stage(i, _):
@@ -330,9 +356,8 @@
         first_copy.wait_send()
 
     def drain(m, _):
-        sent = len(partners) * message_rows
         for source, semaphore in ((dispatched, dispatch_send), (produced, produce_send)):
-            view = source.at[m, pl.ds(0, sent)]
+            view = source.at[m, pl.ds(0, len(partners)), pl.ds(0, sent)]
             pltpu.make_async_copy(view, view, semaphore.at[m]).wait()
 
         @pl.when((section < sections - 1) | (m < micros - 1))
@@ -378,10 +403,10 @@
                 pltpu.VMEM((micros, capacity, rows, experts), F32),
                 pltpu.VMEM((micros, chunks * 16, messages), BF16),
                 pltpu.VMEM((micros, 256, lane), BF16),
-                pltpu.VMEM((micros, messages, lane), BF16),
-                pltpu.VMEM((micros, messages, lane), BF16),
-                pltpu.VMEM((micros, messages, lane), BF16),
-                pltpu.VMEM((micros, messages, lane), BF16),
+                pltpu.VMEM((micros, experts, message_rows, lane), BF16),
+                pltpu.VMEM((micros, experts, message_rows, lane), BF16),
+                pltpu.VMEM((micros, experts, message_rows, lane), BF16),
+                pltpu.VMEM((micros, experts, message_rows, lane), BF16),
                 pltpu.VMEM((slots, width), BF16),
                 pltpu.VMEM((slots, inner_width), BF16),
                 pltpu.VMEM((experts // 4, 256, lane), BF16),
@@ -397,7 +422,7 @@
                 collective_id=0, has_side_effects=True, vmem_limit_bytes=58 * 2**20
             ),
             name="expert_layers",
-        )(tokens, norm_gain, router, w_gate, w_up, w_down, expert_ids)
+        )(tokens, norm_gain, jnp.swapaxes(router, 1, 2), w_gate, w_up, w_down, expert_ids)
 
     placed = (
         P("section", "expert", None),

time: 163 us -> 134 us (0.82)
  Pallas kernels: 159 us -> 132 us
  local copies, waits for them, and re-layouts: 3.62 us -> 1.45 us
    pallas_call x1, Pallas kernels: 159 us -> 132 us  [per_device(): pl.pallas_call(functools.partial(kernel, grid_z, grid_x, sections, chunks...]
    unnamed x2 -> x1, local copies, waits for them, and re-layouts: 3.62 us -> 1.45 us
where the time goes in v2:
time: 134 us
  Pallas kernels  132 us (99%)
  local copies, waits for them, and re-layouts  1.45 us (1%)
    pallas_call x1, Pallas kernels, per_device(): pl.pallas_call(functools.partial(kernel, grid_z, grid_x, sections, chunks...  132 us

profile of v2, /device:TPU:24, one launch (start us, length us, event | category | flops | bytes accessed | tf_op | source)
XLA Modules:
  0.0 133.8 jit_solution(6454555068750274179)
XLA Ops:
  0.0 132.3 %expert_layers.1 = bf16[1,8,3584]{2,1,0:T(8,128)(2,1)} custom-call(bf16[1,8,3584]{2,1,0:T(8,128)(2,1)} %tokens.1, bf16[1,3584]{1,0:T(2,128)(2,1)} %gain.1, bf16[1,32,3584]{2,1,0:T(8,128)(2,1)} %bitcast.1, bf16[1,1,3584,1024]{3,2,1,0:T(8,128)(2,1)} %w_gate.1, bf16[1,1,3584,1024]{3,2,1,0:T(8,128)(2,1)} %w_up.1, bf16[1,1,1024,3584]{3,2,1,0:T(8,128)(2,1)} %w_down.1, ...), custom_call_target="tpu_custom_call" | custom-call | tf_op jit(solution)/shard_map/expert_layers/pallas_call | solution.py:389
  132.3 1.4 %copy.9 = bf16[1,8,3584]{2,1,0:T(8,128)(2,1)} copy(bf16[1,8,3584]{2,1,0:T(8,128)(2,1)} %expert_layers.1) | data formatting | bytes 114688

commit v3 on v2

--- a/solution.py
+++ b/solution.py
@@ -15,7 +15,8 @@
 routed_scale = 2.5
 capacity = 2
 lane = 128
-message_rows = 64
+part_chunks = 16
+part_rows = part_chunks * capacity
 
 
 def dot(a, b):
@@ -44,7 +45,7 @@
     grid_z, grid_x, sections, chunks, tokens, gain, router, w_gate, w_up, w_down, ids, result,
     gate_v, up_v, down_v, hidden, finished, staged, outgoing,
     place, pick, factors, stacked, dispatched, arrived, produced, returned,
-    rows_in, inner, columns, select, select_t, spread, mask_j,
+    rows_in, gate_sum, up_sum, inner, columns, select, select_t, spread, mask_j,
     gate_sem, up_sem, down_sem, hidden_sem, hidden_send, finished_sem,
     dispatch_send, arrive_sem, produce_send, return_sem, local_sem,
 ):
@@ -76,9 +77,12 @@
     copy_up.start()
     copy_down.start()
 
+    parts = [(0, part_chunks), (part_chunks, chunks)]
+    sent = [(last - first) * capacity for first, last in parts]
+
     for room in (arrived, returned):
         for m in range(micros):
-            room[m, :, message_rows - 16 :, :] = jnp.zeros((experts, 16, lane), BF16)
+            room[m, 1, :, part_rows - 16 :, :] = jnp.zeros((experts, 16, lane), BF16)
 
     barrier = pltpu.get_barrier_semaphore()
     for partner in partners:
@@ -88,18 +92,17 @@
             barrier, inc=1, device_id={"section": lax.rem(section + step, sections)}, device_id_type=MESH
         )
 
-    used = chunks * rows
-    sent = chunks * capacity
+    tail = (chunks - part_chunks) * rows
     for m in range(micros):
-        stacked[m, used:, :] = jnp.zeros((256 - used, lane), BF16)
-
-    shape = (message_rows, 256)
+        stacked[m, tail:, lane:] = jnp.zeros((part_chunks * rows - tail, lane), BF16)
+
+    shape = (part_rows, lane)
     r, c = iota(shape, 0), iota(shape, 1)
     diagonal = [
-        jnp.where((c // rows == r // capacity) & (r % capacity == p) & (r < sent), 1.0, 0.0).astype(F32)
+        jnp.where((c // rows == r // capacity) & (r % capacity == p), 1.0, 0.0).astype(F32)
         for p in range(capacity)
     ]
-    repeat = jnp.where(iota((rows, 256), 1) % rows == iota((rows, 256), 0), 1.0, 0.0).astype(F32)
+    repeat = jnp.where(iota((rows, lane), 1) % rows == iota((rows, lane), 0), 1.0, 0.0).astype(F32)
     token_of = iota((rows, experts), 0)
     expert_of = iota((rows, experts), 1)
 
@@ -120,7 +123,7 @@
             )
         for e in range(experts):
             block = diagonal[0] * lanes[0][e : e + 1, :] + diagonal[1] * lanes[1][e : e + 1, :]
-            place[m, e * message_rows : (e + 1) * message_rows, :] = block.astype(BF16)
+            place[m, e * part_rows : (e + 1) * part_rows, :] = block.astype(BF16)
         return 0
 
     def load_hidden(m):
@@ -134,24 +137,35 @@
 
     def fill_slots(m):
         normed = normalize(m)
-        stacked[m, :used, :] = jnp.concatenate(
-            [normed[:, j * lane : (j + 1) * lane] for j in range(chunks)], axis=0
-        ).astype(BF16)
-        dispatched[m] = dot(place[m], stacked[m]).astype(BF16).reshape(experts, message_rows, lane)
-
-    def send_slots(m):
+        for q, (first, last) in enumerate(parts):
+            stacked[m, : (last - first) * rows, q * lane : (q + 1) * lane] = jnp.concatenate(
+                [normed[:, j * lane : (j + 1) * lane] for j in range(first, last)], axis=0
+            ).astype(BF16)
+        slots = dot(place[m], stacked[m]).astype(BF16)
+        for q in range(2):
+            dispatched[m, q] = slots[:, q * lane : (q + 1) * lane].reshape(experts, part_rows, lane)
+
+    def send(m, q, source, target, send_sem, receive_sem):
         for partner in partners:
             pltpu.make_async_remote_copy(
-                src_ref=dispatched.at[m, partner, pl.ds(0, sent)],
-                dst_ref=arrived.at[m, me, pl.ds(0, sent)],
-                send_sem=dispatch_send.at[m], recv_sem=arrive_sem.at[m],
+                src_ref=source.at[m, q, partner, pl.ds(0, sent[q])],
+                dst_ref=target.at[m, q, me, pl.ds(0, sent[q])],
+                send_sem=send_sem.at[m, q], recv_sem=receive_sem.at[m, q],
                 device_id={"expert": partner}, device_id_type=MESH,
             ).start()
         pltpu.make_async_copy(
-            dispatched.at[m, me, pl.ds(0, sent)],
-            arrived.at[m, me, pl.ds(0, sent)],
-            arrive_sem.at[m],
+            source.at[m, q, me, pl.ds(0, sent[q])],
+            target.at[m, q, me, pl.ds(0, sent[q])],
+            receive_sem.at[m, q],
         ).start()
+
+    def receive(m, q, target, receive_sem):
+        view = target.at[m, q, :, pl.ds(0, sent[q])]
+        pltpu.make_async_copy(view, view, receive_sem.at[m, q]).wait()
+
+    def send_slots(m):
+        for q in range(2):
+            send(m, q, dispatched, arrived, dispatch_send, arrive_sem)
 
     def spread_factors(m):
         normed = normalize(m)
@@ -173,10 +187,10 @@
             part = dot(both, spread[p])
             wide = part if wide is None else wide + part
         wide = wide.astype(BF16)
-        for j in range(chunks):
+        for j in range(part_chunks):
             mask = mask_j[j * 16 : (j + 1) * 16, :]
             factors[m, j * 16 : (j + 1) * 16, :] = wide * jnp.concatenate(
-                [mask] * (experts * message_rows // lane), axis=1
+                [mask] * (experts * part_rows // lane), axis=1
             )
 
     def dispatch(m):
@@ -188,19 +202,24 @@
 
         spread_factors(m)
 
+    def sort_rows(m, q):
+        first, last = parts[q]
+        for pair in range(experts // 16):
+            both = [
+                arrived[m, q, 16 * pair + 8 * i : 16 * pair + 8 * i + 8].reshape(8 * part_rows, lane)
+                for i in range(2)
+            ]
+            ordered = dot(select[: (last - first) * 16, :], jnp.concatenate(both, axis=1)).astype(BF16)
+            for j in range(first, last):
+                tile = ordered[(j - first) * 16 : (j - first + 1) * 16, :]
+                cols = slice(j * lane, (j + 1) * lane)
+                rows_in[pair * 32 : pair * 32 + 16, cols] = tile[:, :lane]
+                rows_in[pair * 32 + 16 : pair * 32 + 32, cols] = tile[:, lane:]
+
     def run_experts(m):
-        view = arrived.at[m, :, pl.ds(0, sent)]
-        pltpu.make_async_copy(view, view, arrive_sem.at[m]).wait()
-        group = 4 * message_rows
-        for pair in range(experts // 8):
-            first = arrived[m, 8 * pair : 8 * pair + 4].reshape(group, lane)
-            second = arrived[m, 8 * pair + 4 : 8 * pair + 8].reshape(group, lane)
-            sorted_rows = dot(select[...], jnp.concatenate([first, second], axis=1))
-            for j in range(chunks):
-                tile = sorted_rows[j * 8 : (j + 1) * 8, :]
-                rows_in[pair * 16 : (pair + 1) * 16, j * lane : (j + 1) * lane] = jnp.concatenate(
-                    [tile[:, :lane], tile[:, lane:]], axis=0
-                ).astype(BF16)
+        split = part_chunks * lane
+        receive(m, 0, arrived, arrive_sem)
+        sort_rows(m, 0)
 
         @pl.when(m == 0)
         def _():
@@ -209,8 +228,14 @@
 
         for n in range(inner_width // 256):
             cols = slice(n * 256, (n + 1) * 256)
-            gate_part = dot(rows_in[...], gate_v[:, cols])
-            up_part = dot(rows_in[...], up_v[:, cols])
+            gate_sum[:, cols] = dot(rows_in[:, :split], gate_v[:split, cols])
+            up_sum[:, cols] = dot(rows_in[:, :split], up_v[:split, cols])
+        receive(m, 1, arrived, arrive_sem)
+        sort_rows(m, 1)
+        for n in range(inner_width // 256):
+            cols = slice(n * 256, (n + 1) * 256)
+            gate_part = gate_sum[:, cols] + dot(rows_in[:, split:], gate_v[split:, cols])
+            up_part = up_sum[:, cols] + dot(rows_in[:, split:], up_v[split:, cols])
             inner[:, cols] = (gate_part / (1.0 + jnp.exp(-gate_part)) * up_part).astype(BF16)
 
         @pl.when(m == 0)
@@ -218,38 +243,34 @@
             copy_down.wait()
 
         step = 4
-        for n in range(chunks // step):
-            out = dot(inner[...], down_v[:, n * step * lane : (n + 1) * step * lane])
-            for g in range(experts // 4):
-                columns[g, n * step * 8 : (n + 1) * step * 8, :] = jnp.concatenate(
-                    [out[g * 8 : (g + 1) * 8, j * lane : (j + 1) * lane] for j in range(step)], axis=0
-                ).astype(BF16)
-        for pair in range(experts // 8):
-            both = jnp.concatenate([columns[2 * pair], columns[2 * pair + 1]], axis=1)
-            back = dot(select_t[...], both).astype(BF16)
-            produced[m, 8 * pair : 8 * pair + 4] = back[:, :lane].reshape(4, message_rows, lane)
-            produced[m, 8 * pair + 4 : 8 * pair + 8] = back[:, lane:].reshape(4, message_rows, lane)
-        for partner in partners:
-            pltpu.make_async_remote_copy(
-                src_ref=produced.at[m, partner, pl.ds(0, sent)],
-                dst_ref=returned.at[m, me, pl.ds(0, sent)],
-                send_sem=produce_send.at[m], recv_sem=return_sem.at[m],
-                device_id={"expert": partner}, device_id_type=MESH,
-            ).start()
-        pltpu.make_async_copy(
-            produced.at[m, me, pl.ds(0, sent)],
-            returned.at[m, me, pl.ds(0, sent)],
-            return_sem.at[m],
-        ).start()
+        for q, (first, last) in enumerate(parts):
+            for n in range(first, last, step):
+                out = dot(inner[...], down_v[:, n * lane : (n + step) * lane]).astype(BF16)
+                for g in range(experts // 8):
+                    for j in range(step):
+                        columns[q, g, (n - first + j) * 16 : (n - first + j + 1) * 16, :] = out[
+                            g * 16 : (g + 1) * 16, j * lane : (j + 1) * lane
+                        ]
+            for pair in range(experts // 16):
+                both = jnp.concatenate([columns[q, 2 * pair], columns[q, 2 * pair + 1]], axis=1)
+                back = dot(select_t[...], both).astype(BF16)
+                for i in range(2):
+                    produced[m, q, 16 * pair + 8 * i : 16 * pair + 8 * i + 8] = back[
+                        :, i * lane : (i + 1) * lane
+                    ].reshape(8, part_rows, lane)
+            send(m, q, produced, returned, produce_send, return_sem)
 
     def combine(m):
-        view = returned.at[m, :, pl.ds(0, sent)]
-        pltpu.make_async_copy(view, view, return_sem.at[m]).wait()
-        branch = dot(factors[m], returned[m].reshape(experts * message_rows, lane))
+        for q in range(2):
+            receive(m, q, returned, return_sem)
+        both = [returned[m, q].reshape(experts * part_rows, lane) for q in range(2)]
+        branch = dot(factors[m], jnp.concatenate(both, axis=1))
         values = load_hidden(m)
         fresh = []
         for j in range(chunks):
-            part = branch[j * 16 : j * 16 + 8, :] + branch[j * 16 + 8 : j * 16 + 16, :]
+            q, row = j // part_chunks, (j % part_chunks) * 16
+            cols = slice(q * lane, (q + 1) * lane)
+            part = branch[row : row + 8, cols] + branch[row + 8 : row + 16, cols]
             fresh.append(values[:, j * lane : (j + 1) * lane] + part)
         split = chunks // 2
         outgoing[m] = jnp.concatenate(
@@ -300,24 +321,19 @@
     def _():
         first_copy.start()
 
-    shape = (used, 4 * message_rows)
+    shape = (8 * part_rows, 8 * part_rows)
     r, c = iota(shape, 0), iota(shape, 1)
-    select[...] = ones_where(c == ((r % 8) // 2) * message_rows + (r // 8) * 2 + r % 2)
-    shape = (4 * message_rows, 256)
-    r, c = iota(shape, 0), iota(shape, 1)
-    select_t[...] = ones_where(
-        (c < used) & (r == ((c % 8) // 2) * message_rows + (c // 8) * 2 + c % 2)
-    )
-    shape = (experts, experts * message_rows)
+    select[...] = ones_where(c == ((r % 16) // 2) * part_rows + (r // 16) * 2 + r % 2)
+    select_t[...] = ones_where(r == ((c % 16) // 2) * part_rows + (c // 16) * 2 + c % 2)
+    shape = (experts, experts * part_rows)
     r, c = iota(shape, 0), iota(shape, 1)
     for p in range(capacity):
-        spread[p] = ones_where((c // message_rows == r) & (c % capacity == p))
-    shape = (chunks * 16, lane)
+        spread[p] = ones_where((c // part_rows == r) & (c % capacity == p))
+    shape = (part_chunks * 16, lane)
     r, c = iota(shape, 0), iota(shape, 1)
-    mask_j[...] = ones_where((c % message_rows) // capacity == r // 16)
-    for g in range(experts // 4):
-        columns[g, used:, :] = jnp.zeros((256 - used, lane), BF16)
-
+    mask_j[...] = ones_where((c % part_rows) // capacity == r // 16)
+    for g in range(experts // 8):
+        columns[1, g, (chunks - part_chunks) * 16 :, :] = jnp.zeros(((2 * part_chunks - chunks) * 16, lane), BF16)
     lax.fori_loop(1, micros, plan, 0)
 
     order = schedule(micros)
@@ -356,9 +372,10 @@
         first_copy.wait_send()
 
     def drain(m, _):
-        for source, semaphore in ((dispatched, dispatch_send), (produced, produce_send)):
-            view = source.at[m, pl.ds(0, len(partners)), pl.ds(0, sent)]
-            pltpu.make_async_copy(view, view, semaphore.at[m]).wait()
+        for q in range(2):
+            for source, semaphore in ((dispatched, dispatch_send), (produced, produce_send)):
+                view = source.at[m, q, pl.ds(0, len(partners)), pl.ds(0, sent[q])]
+                pltpu.make_async_copy(view, view, semaphore.at[m, q]).wait()
 
         @pl.when((section < sections - 1) | (m < micros - 1))
         def _():
@@ -379,9 +396,8 @@
         inner_width = w_gate.shape[3]
         chunks = width // lane
         micros = expert_ids.shape[1]
-        used = chunks * rows
         slots = experts * capacity
-        messages = experts * message_rows
+        messages = experts * part_rows
         vmem = pl.BlockSpec(memory_space=pltpu.VMEM)
         anywhere = pl.BlockSpec(memory_space=pl.ANY)
         dma = pltpu.SemaphoreType.DMA
@@ -399,24 +415,26 @@
                 pltpu.VMEM(packed, BF16),
                 pltpu.VMEM(packed, BF16),
                 pltpu.VMEM((micros,) + packed, BF16),
-                pltpu.VMEM((micros, messages, 256), BF16),
+                pltpu.VMEM((micros, messages, lane), BF16),
                 pltpu.VMEM((micros, capacity, rows, experts), F32),
-                pltpu.VMEM((micros, chunks * 16, messages), BF16),
-                pltpu.VMEM((micros, 256, lane), BF16),
-                pltpu.VMEM((micros, experts, message_rows, lane), BF16),
-                pltpu.VMEM((micros, experts, message_rows, lane), BF16),
-                pltpu.VMEM((micros, experts, message_rows, lane), BF16),
-                pltpu.VMEM((micros, experts, message_rows, lane), BF16),
+                pltpu.VMEM((micros, part_chunks * 16, messages), BF16),
+                pltpu.VMEM((micros, part_chunks * rows, 2 * lane), BF16),
+                pltpu.VMEM((micros, 2, experts, part_rows, lane), BF16),
+                pltpu.VMEM((micros, 2, experts, part_rows, lane), BF16),
+                pltpu.VMEM((micros, 2, experts, part_rows, lane), BF16),
+                pltpu.VMEM((micros, 2, experts, part_rows, lane), BF16),
                 pltpu.VMEM((slots, width), BF16),
+                pltpu.VMEM((slots, inner_width), F32),
+                pltpu.VMEM((slots, inner_width), F32),
                 pltpu.VMEM((slots, inner_width), BF16),
-                pltpu.VMEM((experts // 4, 256, lane), BF16),
-                pltpu.VMEM((used, 4 * message_rows), BF16),
-                pltpu.VMEM((4 * message_rows, 256), BF16),
+                pltpu.VMEM((2, experts // 8, part_chunks * 16, lane), BF16),
+                pltpu.VMEM((8 * part_rows, 8 * part_rows), BF16),
+                pltpu.VMEM((8 * part_rows, 8 * part_rows), BF16),
                 pltpu.VMEM((capacity, experts, messages), BF16),
-                pltpu.VMEM((chunks * 16, lane), BF16),
+                pltpu.VMEM((part_chunks * 16, lane), BF16),
                 dma, dma, dma,
                 dma((micros,)), dma((micros,)), dma,
-                dma((micros,)), dma((micros,)), dma((micros,)), dma((micros,)), dma,
+                dma((micros, 2)), dma((micros, 2)), dma((micros, 2)), dma((micros, 2)), dma,
             ],
             compiler_params=pltpu.CompilerParams(
                 collective_id=0, has_side_effects=True, vmem_limit_bytes=58 * 2**20

time: 134 us -> 126 us (0.940)
  Pallas kernels: 132 us -> 124 us
    pallas_call x1, Pallas kernels: 132 us -> 124 us  [per_device(): pl.pallas_call(functools.partial(kernel, grid_z, grid_x, sections, chunks...]
where the time goes in v3:
time: 126 us
  Pallas kernels  124 us (98%)
  local copies, waits for them, and re-layouts  1.45 us (1%)
    pallas_call x1, Pallas kernels, per_device(): pl.pallas_call(functools.partial(kernel, grid_z, grid_x, sections, chunks...  124 us

profile of v3, /device:TPU:24, one launch (start us, length us, event | category | flops | bytes accessed | tf_op | source)
XLA Modules:
  0.0 125.9 jit_solution(5119607902483563399)
XLA Ops:
  0.0 124.5 %expert_layers.1 = bf16[1,8,3584]{2,1,0:T(8,128)(2,1)} custom-call(bf16[1,8,3584]{2,1,0:T(8,128)(2,1)} %tokens.1, bf16[1,3584]{1,0:T(2,128)(2,1)} %gain.1, bf16[1,32,3584]{2,1,0:T(8,128)(2,1)} %bitcast.1, bf16[1,1,3584,1024]{3,2,1,0:T(8,128)(2,1)} %w_gate.1, bf16[1,1,3584,1024]{3,2,1,0:T(8,128)(2,1)} %w_up.1, bf16[1,1,1024,3584]{3,2,1,0:T(8,128)(2,1)} %w_down.1, ...), custom_call_target="tpu_custom_call" | custom-call | tf_op jit(solution)/shard_map/expert_layers/pallas_call | solution.py:405
  124.5 1.4 %copy.9 = bf16[1,8,3584]{2,1,0:T(8,128)(2,1)} copy(bf16[1,8,3584]{2,1,0:T(8,128)(2,1)} %expert_layers.1) | data formatting | bytes 114688

commit v4 on v3

--- a/solution.py
+++ b/solution.py
@@ -62,10 +62,13 @@
     def distance(step, size):
         return min(step, size - step)
 
-    offsets = [(dz, dx, dc) for dz in range(grid_z) for dx in range(grid_x) for dc in range(2)]
-    offsets.sort(key=lambda o: -(10 * (distance(o[0], grid_z) + distance(o[1], grid_x)) + o[2]))
+    offsets = [(da, db, dc) for dc in range(2) for da in range(grid_z) for db in range(grid_x)]
+    offsets.sort(key=lambda o: -(distance(o[0], grid_z) + distance(o[1], grid_x)))
     partners = []
-    for dz, dx, dc in offsets[:-1]:
+    for da, db, dc in offsets:
+        if (da, db, dc) == (0, 0, 0):
+            continue
+        dz, dx = jnp.where(core == 0, da, db), jnp.where(core == 0, db, da)
         partners.append(
             lax.rem(z + dz, grid_z) * (2 * grid_x) + lax.rem(x + dx, grid_x) * 2 + lax.rem(core + dc, 2)
         )
@@ -243,7 +246,7 @@
             copy_down.wait()
 
         step = 4
-        for q, (first, last) in enumerate(parts):
+        for q, (first, last) in reversed(list(enumerate(parts))):
             for n in range(first, last, step):
                 out = dot(inner[...], down_v[:, n * lane : (n + step) * lane]).astype(BF16)
                 for g in range(experts // 8):
@@ -261,16 +264,15 @@
             send(m, q, produced, returned, produce_send, return_sem)
 
     def combine(m):
-        for q in range(2):
+        branch = [None, None]
+        for q in (1, 0):
             receive(m, q, returned, return_sem)
-        both = [returned[m, q].reshape(experts * part_rows, lane) for q in range(2)]
-        branch = dot(factors[m], jnp.concatenate(both, axis=1))
+            branch[q] = dot(factors[m], returned[m, q].reshape(experts * part_rows, lane))
         values = load_hidden(m)
         fresh = []
         for j in range(chunks):
             q, row = j // part_chunks, (j % part_chunks) * 16
-            cols = slice(q * lane, (q + 1) * lane)
-            part = branch[row : row + 8, cols] + branch[row + 8 : row + 16, cols]
+            part = branch[q][row : row + 8, :] + branch[q][row + 8 : row + 16, :]
             fresh.append(values[:, j * lane : (j + 1) * lane] + part)
         split = chunks // 2
         outgoing[m] = jnp.concatenate(

time: 126 us -> 124 us (0.984)
  Pallas kernels: 124 us -> 122 us
    pallas_call x1, Pallas kernels: 124 us -> 122 us  [per_device(): pl.pallas_call(functools.partial(kernel, grid_z, grid_x, sections, chunks...]
where the time goes in v4:
time: 124 us
  Pallas kernels  122 us (98%)
  local copies, waits for them, and re-layouts  1.45 us (1%)
    pallas_call x1, Pallas kernels, per_device(): pl.pallas_call(functools.partial(kernel, grid_z, grid_x, sections, chunks...  122 us

profile of v4, /device:TPU:24, one launch (start us, length us, event | category | flops | bytes accessed | tf_op | source)
XLA Modules:
  0.0 123.8 jit_solution(14934079763390418272)
XLA Ops:
  0.0 122.4 %expert_layers.1 = bf16[1,8,3584]{2,1,0:T(8,128)(2,1)} custom-call(bf16[1,8,3584]{2,1,0:T(8,128)(2,1)} %tokens.1, bf16[1,3584]{1,0:T(2,128)(2,1)} %gain.1, bf16[1,32,3584]{2,1,0:T(8,128)(2,1)} %bitcast.1, bf16[1,1,3584,1024]{3,2,1,0:T(8,128)(2,1)} %w_gate.1, bf16[1,1,3584,1024]{3,2,1,0:T(8,128)(2,1)} %w_up.1, bf16[1,1,1024,3584]{3,2,1,0:T(8,128)(2,1)} %w_down.1, ...), custom_call_target="tpu_custom_call" | custom-call | tf_op jit(solution)/shard_map/expert_layers/pallas_call | solution.py:407
  122.4 1.4 %copy.9 = bf16[1,8,3584]{2,1,0:T(8,128)(2,1)} copy(bf16[1,8,3584]{2,1,0:T(8,128)(2,1)} %expert_layers.1) | data formatting | bytes 114688

commit v5 on v4

--- a/solution.py
+++ b/solution.py
@@ -43,7 +43,7 @@
 
 def kernel(
     grid_z, grid_x, sections, chunks, tokens, gain, router, w_gate, w_up, w_down, ids, result,
-    gate_v, up_v, down_v, hidden, finished, staged, outgoing,
+    gate_v, up_v, down_v, hidden_a, hidden_b, finished_a, finished_b, staged_a, staged_b, outgoing_a, outgoing_b,
     place, pick, factors, stacked, dispatched, arrived, produced, returned,
     rows_in, gate_sum, up_sum, inner, columns, select, select_t, spread, mask_j,
     gate_sem, up_sem, down_sem, hidden_sem, hidden_send, finished_sem,
@@ -55,7 +55,6 @@
     micros = sections
     rows = 8
     width = chunks * lane
-    half = width // 2
     inner_width = gate_v.shape[1]
     core, x, z = lax.rem(me, 2), lax.rem(me // 2, grid_x), me // (2 * grid_x)
 
@@ -80,6 +79,8 @@
     copy_up.start()
     copy_down.start()
 
+    hidden, finished = (hidden_a, hidden_b), (finished_a, finished_b)
+    staged, outgoing = (staged_a, staged_b), (outgoing_a, outgoing_b)
     parts = [(0, part_chunks), (part_chunks, chunks)]
     sent = [(last - first) * capacity for first, last in parts]
 
@@ -129,9 +130,19 @@
             place[m, e * part_rows : (e + 1) * part_rows, :] = block.astype(BF16)
         return 0
 
+    def fold(part):
+        middle = part.shape[1] // 2
+        return jnp.concatenate([part[:, :middle], part[:, middle:]], axis=0).astype(BF16)
+
+    def unfold(refs):
+        pieces = []
+        for packed in refs:
+            packed = packed.astype(F32)
+            pieces += [packed[:rows], packed[rows:]]
+        return jnp.concatenate(pieces, axis=1)
+
     def load_hidden(m):
-        packed = hidden[m].astype(F32)
-        return jnp.concatenate([packed[:rows], packed[rows:]], axis=1)
+        return unfold([hidden[q][m] for q in range(2)])
 
     def normalize(m):
         values = load_hidden(m)
@@ -199,7 +210,8 @@
     def dispatch(m):
         @pl.when((section != 0) | (m != 0))
         def _():
-            pltpu.make_async_copy(hidden.at[m], hidden.at[m], hidden_sem.at[m]).wait()
+            for q in (1, 0):
+                pltpu.make_async_copy(hidden[q].at[m], hidden[q].at[m], hidden_sem.at[m, q]).wait()
             fill_slots(m)
             send_slots(m)
 
@@ -264,56 +276,60 @@
             send(m, q, produced, returned, produce_send, return_sem)
 
     def combine(m):
-        branch = [None, None]
         for q in (1, 0):
+            first, last = parts[q]
             receive(m, q, returned, return_sem)
-            branch[q] = dot(factors[m], returned[m, q].reshape(experts * part_rows, lane))
-        values = load_hidden(m)
-        fresh = []
-        for j in range(chunks):
-            q, row = j // part_chunks, (j % part_chunks) * 16
-            part = branch[q][row : row + 8, :] + branch[q][row + 8 : row + 16, :]
-            fresh.append(values[:, j * lane : (j + 1) * lane] + part)
-        split = chunks // 2
-        outgoing[m] = jnp.concatenate(
-            [jnp.concatenate(fresh[:split], axis=1), jnp.concatenate(fresh[split:], axis=1)], axis=0
-        ).astype(BF16)
-
+            branch = dot(factors[m], returned[m, q].reshape(experts * part_rows, lane))
+            values = unfold([hidden[q][m]])
+            fresh = []
+            for j in range(last - first):
+                part = branch[j * 16 : j * 16 + 8, :] + branch[j * 16 + 8 : j * 16 + 16, :]
+                fresh.append(values[:, j * lane : (j + 1) * lane] + part)
+            outgoing[q][m] = fold(jnp.concatenate(fresh, axis=1))
+            pass_on(m, q)
+
+    def pass_on(m, q):
         @pl.when(section < sections - 1)
         def _():
             pltpu.make_async_remote_copy(
-                src_ref=outgoing.at[m], dst_ref=hidden.at[m],
-                send_sem=hidden_send.at[m], recv_sem=hidden_sem.at[m],
+                src_ref=outgoing[q].at[m], dst_ref=hidden[q].at[m],
+                send_sem=hidden_send.at[m, q], recv_sem=hidden_sem.at[m, q],
                 device_id={"section": lax.rem(section + 1, sections)}, device_id_type=MESH,
             ).start()
 
         @pl.when((section == sections - 1) & (m < micros - 1))
         def _():
             pltpu.make_async_remote_copy(
-                src_ref=outgoing.at[m], dst_ref=finished,
-                send_sem=hidden_send.at[m], recv_sem=finished_sem,
+                src_ref=outgoing[q].at[m], dst_ref=finished[q],
+                send_sem=hidden_send.at[m, q], recv_sem=finished_sem.at[q],
                 device_id={"section": lax.rem(m, sections)}, device_id_type=MESH,
             ).start()
 
         @pl.when((section == sections - 1) & (m == micros - 1))
         def _():
-            finished[...] = outgoing[m]
+            finished[q][...] = outgoing[q][m]
 
     held = tokens[0].astype(F32)
-    staged[...] = jnp.concatenate([held[:, :half], held[:, half:]], axis=0).astype(BF16)
+    for q, (first, last) in enumerate(parts):
+        staged[q][...] = fold(held[:, first * lane : last * lane])
     plan(0)
 
     @pl.when(section == 0)
     def _():
-        hidden[0] = staged[...]
+        for q in range(2):
+            hidden[q][0] = staged[q][...]
         fill_slots(0)
 
     pl.semaphore_wait(barrier, len(partners) + sections - 1)
 
-    first_copy = pltpu.make_async_remote_copy(
-        src_ref=staged, dst_ref=hidden.at[section], send_sem=local_sem, recv_sem=hidden_sem.at[section],
-        device_id={"section": 0}, device_id_type=MESH,
-    )
+    first_copies = [
+        pltpu.make_async_remote_copy(
+            src_ref=staged[q], dst_ref=hidden[q].at[section],
+            send_sem=local_sem.at[q], recv_sem=hidden_sem.at[section, q],
+            device_id={"section": 0}, device_id_type=MESH,
+        )
+        for q in range(2)
+    ]
 
     @pl.when(section == 0)
     def _():
@@ -321,7 +337,8 @@
 
     @pl.when(section != 0)
     def _():
-        first_copy.start()
+        for copy in first_copies:
+            copy.start()
 
     shape = (8 * part_rows, 8 * part_rows)
     r, c = iota(shape, 0), iota(shape, 1)
@@ -364,14 +381,15 @@
 
     @pl.when(section < sections - 1)
     def _():
-        pltpu.make_async_copy(finished, finished, finished_sem).wait()
-
-    packed = finished[...].astype(F32)
-    result[0] = jnp.concatenate([packed[:rows], packed[rows:]], axis=1).astype(BF16)
+        for q in range(2):
+            pltpu.make_async_copy(finished[q], finished[q], finished_sem.at[q]).wait()
+
+    result[0] = unfold([finished[q][...] for q in range(2)]).astype(BF16)
 
     @pl.when(section != 0)
     def _():
-        first_copy.wait_send()
+        for copy in first_copies:
+            copy.wait_send()
 
     def drain(m, _):
         for q in range(2):
@@ -381,7 +399,8 @@
 
         @pl.when((section < sections - 1) | (m < micros - 1))
         def _():
-            pltpu.make_async_copy(outgoing.at[m], outgoing.at[m], hidden_send.at[m]).wait()
+            for q in range(2):
+                pltpu.make_async_copy(outgoing[q].at[m], outgoing[q].at[m], hidden_send.at[m, q]).wait()
 
         return 0
 
@@ -403,7 +422,7 @@
         vmem = pl.BlockSpec(memory_space=pltpu.VMEM)
         anywhere = pl.BlockSpec(memory_space=pl.ANY)
         dma = pltpu.SemaphoreType.DMA
-        packed = (2 * rows, width // 2)
+        packed = [(2 * rows, part_chunks * lane // 2), (2 * rows, (width - part_chunks * lane) // 2)]
         return pl.pallas_call(
             functools.partial(kernel, grid_z, grid_x, sections, chunks),
             out_shape=jax.ShapeDtypeStruct(tokens.shape, BF16),
@@ -413,10 +432,14 @@
                 pltpu.VMEM((width, inner_width), BF16),
                 pltpu.VMEM((width, inner_width), BF16),
                 pltpu.VMEM((inner_width, width), BF16),
-                pltpu.VMEM((micros,) + packed, BF16),
-                pltpu.VMEM(packed, BF16),
-                pltpu.VMEM(packed, BF16),
-                pltpu.VMEM((micros,) + packed, BF16),
+                pltpu.VMEM((micros,) + packed[0], BF16),
+                pltpu.VMEM((micros,) + packed[1], BF16),
+                pltpu.VMEM(packed[0], BF16),
+                pltpu.VMEM(packed[1], BF16),
+                pltpu.VMEM(packed[0], BF16),
+                pltpu.VMEM(packed[1], BF16),
+                pltpu.VMEM((micros,) + packed[0], BF16),
+                pltpu.VMEM((micros,) + packed[1], BF16),
                 pltpu.VMEM((micros, messages, lane), BF16),
                 pltpu.VMEM((micros, capacity, rows, experts), F32),
                 pltpu.VMEM((micros, part_chunks * 16, messages), BF16),
@@ -435,8 +458,8 @@
                 pltpu.VMEM((capacity, experts, messages), BF16),
                 pltpu.VMEM((part_chunks * 16, lane), BF16),
                 dma, dma, dma,
-                dma((micros,)), dma((micros,)), dma,
-                dma((micros, 2)), dma((micros, 2)), dma((micros, 2)), dma((micros, 2)), dma,
+                dma((micros, 2)), dma((micros, 2)), dma((2,)),
+                dma((micros, 2)), dma((micros, 2)), dma((micros, 2)), dma((micros, 2)), dma((2,)),
             ],
             compiler_params=pltpu.CompilerParams(
                 collective_id=0, has_side_effects=True, vmem_limit_bytes=58 * 2**20

time: 124 us -> 123 us (level)
  no operation moved by 1% of the time
where the time goes in v5:
time: 123 us
  Pallas kernels  121 us (98%)
  local copies, waits for them, and re-layouts  1.45 us (1%)
    pallas_call x1, Pallas kernels, per_device(): pl.pallas_call(functools.partial(kernel, grid_z, grid_x, sections, chunks...  121 us

profile of v5, /device:TPU:24, one launch (start us, length us, event | category | flops | bytes accessed | tf_op | source)
XLA Modules:
  0.0 122.7 jit_solution(6153191729851514587)
XLA Ops:
  0.0 121.2 %expert_layers.1 = bf16[1,8,3584]{2,1,0:T(8,128)(2,1)} custom-call(bf16[1,8,3584]{2,1,0:T(8,128)(2,1)} %tokens.1, bf16[1,3584]{1,0:T(2,128)(2,1)} %gain.1, bf16[1,32,3584]{2,1,0:T(8,128)(2,1)} %bitcast.1, bf16[1,1,3584,1024]{3,2,1,0:T(8,128)(2,1)} %w_gate.1, bf16[1,1,3584,1024]{3,2,1,0:T(8,128)(2,1)} %w_up.1, bf16[1,1,1024,3584]{3,2,1,0:T(8,128)(2,1)} %w_down.1, ...), custom_call_target="tpu_custom_call" | custom-call | tf_op jit(solution)/shard_map/expert_layers/pallas_call | solution.py:426
  121.2 1.4 %copy.9 = bf16[1,8,3584]{2,1,0:T(8,128)(2,1)} copy(bf16[1,8,3584]{2,1,0:T(8,128)(2,1)} %expert_layers.1) | data formatting | bytes 114688

commit v6 on v5

--- a/solution.py
+++ b/solution.py
@@ -68,6 +68,8 @@
         if (da, db, dc) == (0, 0, 0):
             continue
         dz, dx = jnp.where(core == 0, da, db), jnp.where(core == 0, db, da)
+        odd = lax.rem(x + z, 2) == 1
+        dz, dx = jnp.where(odd, grid_z - dz, dz), jnp.where(odd, grid_x - dx, dx)
         partners.append(
             lax.rem(z + dz, grid_z) * (2 * grid_x) + lax.rem(x + dx, grid_x) * 2 + lax.rem(core + dc, 2)
         )

time: 123 us -> 123 us (level)
  no operation moved by 1% of the time
where the time goes in v6:
time: 123 us
  Pallas kernels  121 us (98%)
  local copies, waits for them, and re-layouts  1.45 us (1%)
    pallas_call x1, Pallas kernels, per_device(): pl.pallas_call(functools.partial(kernel, grid_z, grid_x, sections, chunks...  121 us

profile of v6, /device:TPU:24, one launch (start us, length us, event | category | flops | bytes accessed | tf_op | source)
XLA Modules:
  0.0 122.8 jit_solution(1441983862592181058)
XLA Ops:
  0.0 121.3 %expert_layers.1 = bf16[1,8,3584]{2,1,0:T(8,128)(2,1)} custom-call(bf16[1,8,3584]{2,1,0:T(8,128)(2,1)} %tokens.1, bf16[1,3584]{1,0:T(2,128)(2,1)} %gain.1, bf16[1,32,3584]{2,1,0:T(8,128)(2,1)} %bitcast.1, bf16[1,1,3584,1024]{3,2,1,0:T(8,128)(2,1)} %w_gate.1, bf16[1,1,3584,1024]{3,2,1,0:T(8,128)(2,1)} %w_up.1, bf16[1,1,1024,3584]{3,2,1,0:T(8,128)(2,1)} %w_down.1, ...), custom_call_target="tpu_custom_call" | custom-call | tf_op jit(solution)/shard_map/expert_layers/pallas_call | solution.py:428
  121.3 1.4 %copy.9 = bf16[1,8,3584]{2,1,0:T(8,128)(2,1)} copy(bf16[1,8,3584]{2,1,0:T(8,128)(2,1)} %expert_layers.1) | data formatting | bytes 114688
